TPU v7x, 512 devices: a whole 4x4x16 slice. The times are simulated.
512 devices in a mesh: gx: 8 (over x, core), gy: 4 (over y), gz: 16 (over z).
Axes of the slice: x: 4, y: 4, z: 16, core: 2. Of those that a mesh axis runs over, the one named last changes fastest.
Arguments:
- probes: bfloat16 [48, 3, 8, 8, 2048], P(None, None, 'gx', 'gy', 'gz'), may hold values from -6 to 6
- stiffness: float32 [8, 8, 2048], P('gx', 'gy', 'gz'), may hold values from 0.1 to 10
- diag_tiles: bfloat16 [8, 4, 16, 6, 128, 128], P('gx', 'gy', 'gz'), may hold values from -0.25 to 3.25
- off_tiles: bfloat16 [8, 4, 16, 24, 128, 128], P('gx', 'gy', 'gz'), may hold values from -0.3984375 to 0.3984375
- off_rows: int32 [8, 4, 16, 24], P('gx', 'gy', 'gz'), may hold values from 0 to 5
- off_cols: int32 [8, 4, 16, 24], P('gx', 'gy', 'gz'), may hold values from 0 to 5
- off_count: int32 [8, 4, 16], P('gx', 'gy', 'gz'), may hold values from 12 to 24, as said below
Outputs:
- deflation: bfloat16 [32, 3, 8, 8, 2048], P(None, None, 'gx', 'gy', 'gz')
- coarse_self: float32 [8, 4, 16, 1024], P('gx', 'gy')
- coarse_pairs: float32 [8, 4, 16, 26, 1024], P('gx', 'gy')
Inputs may be any that keep to these rules, and one draw needn't show every extreme that they name: `off_count`: some subdomain has exactly 24 tiles in use.
All inputs are finite; a program needn't handle non-finite values.
Results may differ from a plain program's by a relative error of at most 0.0051.
Values may be sent and summed in bfloat16 or wider, within the bound.
A program may use at most 64 MiB of HBM per device.

v0:
```python
import jax
import jax.numpy as jnp
from jax import lax
from jax.experimental import pallas as pl
from jax.experimental.pallas import tpu as pltpu
from jax.sharding import PartitionSpec as P

MESH = pl.DeviceIdType.MESH
F32 = jnp.float32
BF16 = jnp.bfloat16
HIGHEST = lax.Precision.HIGHEST

DEFL = 32
ITERS = 12
SHIFT = 8.0
TILE = 128
SAFE_PIVOT = 0.01


def iota(shape, dim):
    return lax.broadcasted_iota(jnp.int32, shape, dim)


def dot_nt(a, b, precision=None):
    return lax.dot_general(
        a, b, (((1,), (1,)), ((), ())), preferred_element_type=F32, precision=precision
    )


def weight_kernel(stiff_ref, weight_ref, got, send_sem, recv_sem):
    sizes = [lax.axis_size(a) for a in ("gx", "gy", "gz")]
    here = [lax.axis_index(a) for a in ("gx", "gy", "gz")]
    faces = []
    for dim, size in enumerate(sizes):
        for step in (-1, 1):
            there = list(here)
            there[dim] = lax.rem(here[dim] + step + size, size)
            faces.append(tuple(there))
    barrier = pltpu.get_barrier_semaphore()
    for there in faces:
        pl.semaphore_signal(barrier, inc=1, device_id=there, device_id_type=MESH)
    pl.semaphore_wait(barrier, len(faces))
    copies = []
    for face, there in enumerate(faces):
        copy = pltpu.make_async_remote_copy(
            src_ref=stiff_ref,
            dst_ref=got.at[face ^ 1],
            send_sem=send_sem.at[face],
            recv_sem=recv_sem.at[face ^ 1],
            device_id=there,
            device_id_type=MESH,
        )
        copy.start()
        copies.append(copy)
    for copy in copies:
        copy.wait()
    zero = jnp.zeros(stiff_ref.shape, F32)
    stiff = stiff_ref[...]

    def face_value(face):
        dim, high = face // 2, face % 2
        inside = here[dim] < sizes[dim] - 1 if high else here[dim] > 0
        return jnp.where(inside, got[face], zero)

    total = face_value(1) + face_value(0)
    row = iota(stiff.shape, 0)
    y_low, y_high = face_value(2), face_value(3)
    total = total + jnp.where(row == 0, pltpu.roll(stiff, 1, 0), y_high[0:1, :])
    total = total + jnp.where(row == 1, pltpu.roll(stiff, 1, 0), y_low[1:2, :])
    lane = iota(stiff.shape, 1)
    z_low, z_high = face_value(4), face_value(5)
    width = stiff.shape[1]
    total = total + jnp.where(
        lane == width - 1, z_high[:, 0:1], pltpu.roll(stiff, width - 1, 1)
    )
    total = total + jnp.where(lane == 0, z_low[:, width - 1 : width], pltpu.roll(stiff, 1, 1))
    weight_ref[...] = stiff / (stiff + total / 6.0)


def cell_weights(stiff):
    return pl.pallas_call(
        weight_kernel,
        out_shape=jax.ShapeDtypeStruct(stiff.shape, F32),
        in_specs=[pl.BlockSpec(memory_space=pltpu.VMEM)],
        out_specs=pl.BlockSpec(memory_space=pltpu.VMEM),
        scratch_shapes=[
            pltpu.VMEM((6,) + stiff.shape, F32),
            pltpu.SemaphoreType.DMA((6,)),
            pltpu.SemaphoreType.DMA((6,)),
        ],
        compiler_params=pltpu.CompilerParams(collective_id=0, has_side_effects=True),
        name="cell_weights",
    )(stiff)


def eliminate(gram):
    count = gram.shape[0]
    start = jnp.concatenate([gram, (iota(gram.shape, 0) == iota(gram.shape, 1)).astype(F32)], 1)
    row = iota((count, 1), 0)
    work = start
    pivots = jnp.zeros((count, 1), F32)
    for j in range(count):
        column = work[:, j : j + 1]
        pivot = column[j : j + 1, :]
        factor = jnp.where(row > j, column * (1.0 / pivot), 0.0)
        pivots = jnp.where(row == j, column, pivots)
        work = work - factor * work[j : j + 1, :]
    inverse = work[:, count:] * lax.rsqrt(pivots)
    original = jnp.sum(
        jnp.where(iota(gram.shape, 0) == iota(gram.shape, 1), gram, 0.0), axis=1, keepdims=True
    )
    return inverse, jnp.min(pivots / original)


def split(x):
    high = x.astype(BF16)
    return high, (x - high.astype(F32)).astype(BF16)


def basis_kernel(
    rows_ref, cols_ref, count_ref, probe_ref, weight_ref, diag_ref, off_ref,
    defl_ref, field_ref, self_ref,
    dense, matrix,
):
    tiles = diag_ref.shape[0]
    total = tiles * TILE
    probes = probe_ref.shape[0]
    eye = iota((TILE, TILE), 0) == iota((TILE, TILE), 1)

    dense[...] = jnp.zeros(dense.shape, F32)
    for t in range(tiles):
        dense[t, t] = diag_ref[t].astype(F32)

    def add_tile(m, carry):
        t, u = rows_ref[m], cols_ref[m]
        dense[t, u] = dense[t, u] + off_ref[m].astype(F32)
        return carry

    lax.fori_loop(0, count_ref[0], add_tile, 0)
    level = []
    for t in range(tiles):
        for u in range(tiles):
            block = dense[t, u]
            if t == u:
                level.append(jnp.sum(jnp.where(eye, block, 0.0), axis=0, keepdims=True))
                block = jnp.where(eye, 0.0, block)
            matrix[u * TILE : (u + 1) * TILE, t * TILE : (t + 1) * TILE] = block.T.astype(BF16)
    level = jnp.concatenate(level, axis=1)
    weight = weight_ref[...]
    weight = jnp.concatenate([weight[0:1, :], weight[1:2, :]] * (tiles // 2), axis=1)
    step_weight = weight * (1.0 / SHIFT)

    def apply(high, low):
        both = jnp.dot(
            jnp.concatenate([high, low], axis=0), matrix[...], preferred_element_type=F32
        )
        return both[: high.shape[0]] + both[high.shape[0] :]

    def image_of(basis):
        scaled = basis * weight
        return basis - step_weight * (apply(*split(scaled)) + level * scaled)

    def normaliser(image):
        return eliminate(dot_nt(image, image, HIGHEST) * (1.0 / total))

    def finish(inverse, image):
        kept = jnp.dot(inverse, image, preferred_element_type=F32, precision=HIGHEST)[:DEFL]
        defl_ref[...] = kept.astype(BF16)
        weighted = (kept * weight).astype(BF16)
        for t in range(tiles):
            field_ref[t % 2, :, t // 2 * TILE : (t // 2 + 1) * TILE] = weighted[
                :, t * TILE : (t + 1) * TILE
            ]
        wide = weighted.astype(F32)
        applied = jnp.dot(weighted, matrix[...], preferred_element_type=F32) + level * wide
        high, low = split(applied)
        self_ref[...] = (dot_nt(weighted, high) + dot_nt(weighted, low)) * (1.0 / total)

    image = probe_ref[...].astype(F32)
    for _ in range(ITERS):
        image = image_of(image)
    inverse, least = normaliser(image)
    finish(inverse, image)

    @pl.when(jnp.logical_not(least > SAFE_PIVOT))
    def _():
        def iteration(_, basis):
            image = image_of(basis)
            inverse, _ = normaliser(image)
            return jnp.dot(inverse, image, preferred_element_type=F32, precision=HIGHEST)

        basis = lax.fori_loop(0, ITERS - 1, iteration, probe_ref[...].astype(F32))
        image = image_of(basis)
        inverse, _ = normaliser(image)
        finish(inverse, image)


def local_basis(probes, weight, diagonal, off_block, rows, cols, count):
    tiles = diagonal.shape[0]
    total = tiles * TILE
    smem = pl.BlockSpec(memory_space=pltpu.SMEM)
    vmem = pl.BlockSpec(memory_space=pltpu.VMEM)
    return pl.pallas_call(
        basis_kernel,
        out_shape=(
            jax.ShapeDtypeStruct((DEFL, total), BF16),
            jax.ShapeDtypeStruct((2, DEFL, total // 2), BF16),
            jax.ShapeDtypeStruct((DEFL, DEFL), F32),
        ),
        in_specs=[smem, smem, smem, vmem, vmem, vmem, vmem],
        out_specs=(vmem, vmem, vmem),
        scratch_shapes=[
            pltpu.VMEM((tiles, tiles, TILE, TILE), F32),
            pltpu.VMEM((total, total), BF16),
        ],
        compiler_params=pltpu.CompilerParams(vmem_limit_bytes=24 * 2**20),
        name="local_basis",
    )(rows, cols, count, probes, weight, diagonal, off_block)


PLANE = 9
OWN = 4
PARTS = 16
PAYLOAD_ROWS = 16


def plane_step(m):
    return m // 3 - 1, m % 3 - 1


def end_picker(y, half):
    row, lane = iota((PARTS, half), 0), iota((PARTS, half), 1)
    end, part = row // 8, row % 8
    hit = (part // 3 == y) & (part < 6) & (lane == (part % 3) * TILE + end * (TILE - 1))
    return hit.astype(BF16)


def exchange_kernel(
    field_ref, self_ref, out_ref, full, sides, ring, send_sem, recv_sem, up_send, up_recv,
    down_send, down_recv,
):
    n_x, n_y, n_z = (lax.axis_size(a) for a in ("gx", "gy", "gz"))
    my_x, my_y, my_z = (lax.axis_index(a) for a in ("gx", "gy", "gz"))
    half = field_ref.shape[2]

    def device(m):
        step_x, step_y = plane_step(m)
        return (lax.rem(my_x + step_x + n_x, n_x), lax.rem(my_y + step_y + n_y, n_y), my_z)

    def line(step):
        return (my_x, my_y, lax.rem(my_z + step + n_z, n_z))

    neighbours = [m for m in range(PLANE) if m != OWN]
    barrier = pltpu.get_barrier_semaphore()
    for m in neighbours:
        pl.semaphore_signal(barrier, inc=1, device_id=device(m), device_id_type=MESH)
    for step in (-1, 1):
        pl.semaphore_signal(barrier, inc=1, device_id=line(step), device_id_type=MESH)
    pl.semaphore_wait(barrier, len(neighbours) + 2)

    slot = {m: i for i, m in enumerate(m for m in neighbours if plane_step(m)[1] != 0)}
    copies = []
    for m in neighbours:
        step_x, step_y = plane_step(m)
        back = PLANE - 1 - m
        if step_y == 0:
            source, target = field_ref, full.at[back // 3 // 2]
        else:
            source, target = field_ref.at[1 if step_y > 0 else 0], sides.at[slot[back]]
        copy = pltpu.make_async_remote_copy(
            src_ref=source,
            dst_ref=target,
            send_sem=send_sem.at[m],
            recv_sem=recv_sem.at[back],
            device_id=device(m),
            device_id_type=MESH,
        )
        copy.start()
        copies.append(copy)

    pick = [end_picker(y, half) for y in range(2)]
    own = [field_ref[y] for y in range(2)]
    stack = [[jnp.concatenate([-own[y], pick[z]], axis=0) for z in range(2)] for y in range(2)]
    spread = (iota((DEFL, DEFL * DEFL), 1) % DEFL == iota((DEFL, DEFL * DEFL), 0)).astype(BF16)
    for copy in copies:
        copy.wait_recv()

    parts = []
    for m in range(PLANE):
        step_x, step_y = plane_step(m)
        if m == OWN:
            ends = dot_nt(pick[0], own[0]) + dot_nt(pick[1], own[1])
            parts.append(jnp.concatenate([self_ref[...], ends], axis=0))
            continue
        if step_y == 0:
            side = m // 3 // 2
            block = dot_nt(stack[0][0], full[side, 0]) + dot_nt(stack[1][1], full[side, 1])
        elif step_y < 0:
            block = dot_nt(stack[0][1], sides[slot[m]])
        else:
            block = dot_nt(stack[1][0], sides[slot[m]])
        inside = True
        if step_x != 0:
            inside = my_x < n_x - 1 if step_x > 0 else my_x > 0
        if step_y != 0:
            inside = jnp.logical_and(inside, my_y < n_y - 1 if step_y > 0 else my_y > 0)
        parts.append(jnp.where(inside, block, 0.0))
    parts = jnp.concatenate(parts, axis=0).astype(BF16)

    group = DEFL + PARTS
    rows = PLANE * group
    wide = jnp.dot(parts, spread, preferred_element_type=F32)
    row = iota((rows, 1), 0)
    m, r = row // group, row % group
    place = jnp.where(r < DEFL, r, (PARTS * m + r - DEFL) % DEFL)
    lane_group = iota((rows, DEFL * DEFL), 1) // DEFL
    wide = jnp.where(lane_group == place, wide, 0.0).astype(BF16)
    column = iota((PAYLOAD_ROWS, rows), 1)
    m, r = column // group, column % group
    target = jnp.where(r < DEFL, m, PLANE + (PARTS * m + r - DEFL) // DEFL)
    gather = (target == iota((PAYLOAD_ROWS, rows), 0)).astype(BF16)
    ring[my_z] = jnp.dot(gather, wide, preferred_element_type=F32).astype(BF16)

    steps_up = n_z // 2
    steps_down = n_z - 1 - steps_up

    def hop(owner, step, sends, recvs, t):
        return pltpu.make_async_remote_copy(
            src_ref=ring.at[owner],
            dst_ref=ring.at[owner],
            send_sem=sends.at[t],
            recv_sem=recvs.at[t],
            device_id=line(step),
            device_id_type=MESH,
        )

    hops = []
    for t in range(steps_up):
        up = hop(lax.rem(my_z - t + n_z, n_z), 1, up_send, up_recv, t)
        up.start()
        hops.append(up)
        if t < steps_down:
            down = hop(lax.rem(my_z + t, n_z), -1, down_send, down_recv, t)
            down.start()
            hops.append(down)
        up.wait_recv()
        if t < steps_down:
            down.wait_recv()
    for copy in copies + hops:
        copy.wait_send()
    out_ref[...] = ring[...]


def exchange(field, self_block, n_z):
    vmem = pl.BlockSpec(memory_space=pltpu.VMEM)
    dma = pltpu.SemaphoreType.DMA
    half = field.shape[2]
    payload = (n_z, PAYLOAD_ROWS, DEFL * DEFL)
    return pl.pallas_call(
        exchange_kernel,
        out_shape=jax.ShapeDtypeStruct(payload, BF16),
        in_specs=[vmem, vmem],
        out_specs=vmem,
        scratch_shapes=[
            pltpu.VMEM((2, 2, DEFL, half), BF16),
            pltpu.VMEM((6, DEFL, half), BF16),
            pltpu.VMEM(payload, BF16),
            dma((PLANE,)),
            dma((PLANE,)),
            dma((n_z // 2,)),
            dma((n_z // 2,)),
            dma((n_z // 2,)),
            dma((n_z // 2,)),
        ],
        compiler_params=pltpu.CompilerParams(
            collective_id=1, has_side_effects=True, vmem_limit_bytes=24 * 2**20
        ),
        name="exchange",
    )(field, self_block)


def pair_index(m, step_z):
    flat = 3 * m + step_z + 1
    return flat if flat < 13 else flat - 1


def unpack_kernel(gathered_ref, self_ref, pairs_ref):
    n_z = self_ref.shape[0]
    width = DEFL * DEFL
    packed = gathered_ref[...]
    cells = n_z * PAYLOAD_ROWS
    column = iota((1, cells), 1)

    def select(rows, shift):
        index = iota((len(rows) * n_z, 1), 0)
        member = index % n_z + shift
        wanted = jnp.full(index.shape, rows[0], jnp.int32)
        for i in range(1, len(rows)):
            wanted = jnp.where(index // n_z == i, rows[i], wanted)
        inside = (member >= 0) & (member < n_z)
        wanted = jnp.where(inside, member * PAYLOAD_ROWS + wanted, -1)
        hit = (column == wanted).astype(BF16)
        return jnp.dot(hit, packed, preferred_element_type=F32)

    blocks = select(list(range(PLANE)), 0)
    for m in range(PLANE):
        block = blocks[m * n_z : (m + 1) * n_z]
        if m == OWN:
            self_ref[...] = block
        else:
            pairs_ref[pair_index(m, 0)] = block

    per_tile = TILE // DEFL
    own_row = PLANE + OWN * PARTS // DEFL
    own_tiles = select([own_row], 0).astype(BF16)
    own_tiles = jnp.concatenate(
        [own_tiles[:, i * TILE : (i + 1) * TILE] for i in range(PARTS // per_tile)], axis=0
    )
    value, lane = iota((TILE, width), 0), iota((TILE, width), 1)
    own = []
    for v in range(per_tile):
        spread = jnp.where(value == v * DEFL + lane // DEFL, -1.0, 0.0).astype(BF16)
        own.append(jnp.dot(own_tiles, spread, preferred_element_type=F32))

    def own_part(part):
        i = part // per_tile
        return own[part % per_tile][i * n_z : (i + 1) * n_z]

    value, lane = iota((TILE, per_tile * TILE), 0), iota((TILE, per_tile * TILE), 1)
    repeat = (value == lane // TILE * DEFL + lane % DEFL).astype(BF16)
    end_rows = list(range(PLANE, PLANE + (PLANE * PARTS + DEFL - 1) // DEFL))
    for step_z in (-1, 1):
        rows = select(end_rows, step_z).astype(BF16)
        first = 0 if step_z > 0 else 2
        tiles = [first, first + 1, first + 4, first + 5]
        stacked = jnp.concatenate([rows[:, i * TILE : (i + 1) * TILE] for i in tiles], axis=0)
        theirs = jnp.dot(stacked, repeat, preferred_element_type=F32)

        def their_part(m, part):
            block = (m % 2) * 2 + part // per_tile
            start = (block * len(end_rows) + m // 2) * n_z
            v = part % per_tile
            return theirs[start : start + n_z, v * TILE : (v + 1) * TILE]

        own_end = 8 if step_z > 0 else 0
        for m in range(PLANE):
            step_y = plane_step(m)[1]
            pairs = [(0, 0), (1, 1)] if step_y == 0 else [(0, 1)] if step_y < 0 else [(1, 0)]
            total = None
            for own_y, their_y in pairs:
                for c in range(3):
                    left = own_part(own_end + own_y * 3 + c)
                    right = jnp.concatenate([their_part(m, their_y * 3 + c)] * (width // TILE), 1)
                    term = left * right
                    total = term if total is None else total + term
            pairs_ref[pair_index(m, step_z)] = total


def unpack(gathered, n_z):
    vmem = pl.BlockSpec(memory_space=pltpu.VMEM)
    width = DEFL * DEFL
    return pl.pallas_call(
        unpack_kernel,
        out_shape=(
            jax.ShapeDtypeStruct((n_z, width), F32),
            jax.ShapeDtypeStruct((26, n_z, width), F32),
        ),
        in_specs=[vmem],
        out_specs=(vmem, vmem),
        compiler_params=pltpu.CompilerParams(vmem_limit_bytes=32 * 2**20),
        name="unpack",
    )(gathered.reshape(n_z * PAYLOAD_ROWS, width))


def per_device(probes, stiffness, diag_tiles, off_tiles, off_rows, off_cols, off_count):
    n_z = lax.axis_size("gz")
    cell_shape = probes.shape[1:]
    weight = cell_weights(stiffness[0])
    deflation, field, self_block = local_basis(
        probes.reshape(probes.shape[0], -1),
        weight,
        diag_tiles[0, 0, 0],
        off_tiles[0, 0, 0],
        off_rows[0, 0, 0],
        off_cols[0, 0, 0],
        off_count[0, 0],
    )
    gathered = exchange(field, self_block, n_z)
    coarse_self, coarse_pairs = unpack(gathered, n_z)
    return (
        deflation.reshape((DEFL,) + cell_shape),
        coarse_self[None, None],
        coarse_pairs.transpose(1, 0, 2)[None, None],
    )


def solution(mesh):
    placed = (
        P(None, None, "gx", "gy", "gz"),
        P("gx", "gy", "gz"),
        P("gx", "gy", "gz", None, None, None),
        P("gx", "gy", "gz", None, None, None),
        P("gx", "gy", "gz", None),
        P("gx", "gy", "gz", None),
        P("gx", "gy", "gz"),
    )
    return jax.shard_map(
        per_device,
        mesh=mesh,
        in_specs=placed,
        out_specs=(
            P(None, None, "gx", "gy", "gz"),
            P("gx", "gy", None, None),
            P("gx", "gy", None, None, None),
        ),
        check_vma=False,
    )
```

profile of v0, /device:TPU:8, one launch (start us, length us, event | category | flops | bytes accessed | tf_op | source)
XLA Modules:
  0.0 72.4 jit_solution(2437240362392792264)
XLA Ops:
  1.3 15.4 %cell_weights.1.weight_ref = f32[2,128]{1,0:T(2,128)} custom-call(f32[2,128]{1,0:T(2,128)} %bitcast.19), custom_call_target="tpu_custom_call" | custom-call | tf_op jit(solution)/shard_map/cell_weights/pallas_call | solution.py:81
  16.7 0.9 %reshape.15.probe_ref = bf16[48,768]{1,0:T(8,128)(2,1)S(1)} reshape(bf16[48,3,1,2,128]{4,3,2,1,0:T(2,128)(2,1)} %param.7) | data formatting | bytes 147456 | tf_op jit(solution)/shard_map/reshape | solution.py:480
  17.6 0.0 copy-start
  17.6 1.1 %copy-done = bf16[1,1,1,24,128,128]{5,4,3,2,1,0:T(8,128)(2,1)S(1)} copy-done((bf16[1,1,1,24,128,128]{5,4,3,2,1,0:T(8,128)(2,1)S(1)}, bf16[1,1,1,24,128,128]{5,4,3,2,1,0:T(8,128)(2,1)}, u32[]{:S(2)}) %copy-start) | copy-done | bytes 786456
  18.7 0.0 copy-start.1
  18.7 0.9 %copy-done.1 = bf16[1,1,1,6,128,128]{5,4,3,2,1,0:T(8,128)(2,1)S(1)} copy-done((bf16[1,1,1,6,128,128]{5,4,3,2,1,0:T(8,128)(2,1)S(1)}, bf16[1,1,1,6,128,128]{5,4,3,2,1,0:T(8,128)(2,1)}, u32[]{:S(2)}) %copy-start.1) | copy-done | bytes 196632
  19.7 0.0 copy-start.2
  19.7 0.7 copy-done.2
  20.3 0.0 copy-start.3
  20.3 0.7 copy-done.3
  21.0 0.0 copy-start.4
  21.0 0.7 copy-done.4
  21.7 9.6 %local_basis.1 = (bf16[32,768]{1,0:T(8,128)(2,1)S(1)}, bf16[2,32,384]{2,1,0:T(8,128)(2,1)S(1)}, f32[32,32]{1,0:T(8,128)S(1)}) custom-call(s32[24]{0:T(128)S(1)} %bitcast.16, s32[24]{0:T(128)S(1)} %bitcast.17, s32[1]{0:T(128)} %bitcast.12.count_ref, bf16[48,768]{1,0:T(8,128)(2,1)S(1)} %reshape.15.probe_ref, f32[2,128]{1,0:T(2,128)S(1)} %copy-done.2, ...), custom_call_target="tpu_custom_call" | custom-call | tf_op jit(solution)/shard_map/local_basis/pallas_call | solution.py:203
  31.2 0.7 reshape.16
  31.9 38.2 %exchange.1 = bf16[16,16,1024]{2,1,0:T(8,128)(2,1)S(1)} custom-call(bf16[2,32,384]{2,1,0:T(8,128)(2,1)S(1)} %get-tuple-element.9.field_ref, f32[32,32]{1,0:T(8,128)S(1)} %get-tuple-element.10.self_ref), custom_call_target="tpu_custom_call" | custom-call | tf_op jit(solution)/shard_map/exchange/pallas_call | solution.py:359
  70.0 2.3 %unpack.1 = (f32[16,1024]{1,0:T(8,128)}, f32[26,16,1024]{2,1,0:T(8,128)}) custom-call(bf16[256,1024]{1,0:T(8,128)(2,1)S(1)} %bitcast.13), custom_call_target="tpu_custom_call" | custom-call | tf_op jit(solution)/shard_map/unpack/pallas_call | solution.py:462
Async XLA Ops:
  17.6 1.1 %copy-start = (bf16[1,1,1,24,128,128]{5,4,3,2,1,0:T(8,128)(2,1)S(1)}, bf16[1,1,1,24,128,128]{5,4,3,2,1,0:T(8,128)(2,1)}, u32[]{:S(2)}) copy-start(bf16[1,1,1,24,128,128]{5,4,3,2,1,0:T(8,128)(2,1)} %param.10) | copy-start | bytes 2359300
  18.7 0.9 %copy-start.1 = (bf16[1,1,1,6,128,128]{5,4,3,2,1,0:T(8,128)(2,1)S(1)}, bf16[1,1,1,6,128,128]{5,4,3,2,1,0:T(8,128)(2,1)}, u32[]{:S(2)}) copy-start(bf16[1,1,1,6,128,128]{5,4,3,2,1,0:T(8,128)(2,1)} %param.9) | copy-start | bytes 589828
  19.7 0.7 copy-start.2
  20.3 0.7 copy-start.3
  21.0 0.7 copy-start.4
where the time goes:
time: 72.7 us; the launch traced here: 72.4 us
  Pallas kernels  65.4 us (90%)
  local copies, waits for them, and re-layouts  5.63 us (8%)
  between operations  1.31 us (2%)
    pallas_call x1, Pallas kernels, exchange(): pl.pallas_call(exchange_kernel, out_shape=jax.ShapeDtypeStruct(payload, B...  38.2 us
    pallas_call x1, Pallas kernels, cell_weights(): pl.pallas_call(weight_kernel, out_shape=jax.ShapeDtypeStruct(stiff.shape,...  15.4 us
    pallas_call x1, Pallas kernels, local_basis(): pl.pallas_call(basis_kernel, out_shape=(jax.ShapeDtypeStruct((DEFL, total...  9.55 us
    unnamed x10, local copies, waits for them, and re-layouts  4.04 us
    pallas_call x1, Pallas kernels, unpack(): pl.pallas_call(unpack_kernel, out_shape=(jax.ShapeDtypeStruct((n_z, width...  2.31 us

commit v1 on v0

v1 whole, which is shorter than its diff:
```python
import jax
import jax.numpy as jnp
from jax import lax
from jax.experimental import pallas as pl
from jax.experimental.pallas import tpu as pltpu
from jax.sharding import PartitionSpec as P

MESH = pl.DeviceIdType.MESH
F32 = jnp.float32
BF16 = jnp.bfloat16
HIGHEST = lax.Precision.HIGHEST

DEFL = 32
ITERS = 12
SHIFT = 8.0
TILE = 128
SAFE_PIVOT = 0.01


def iota(shape, dim):
    return lax.broadcasted_iota(jnp.int32, shape, dim)


def dot_nt(a, b, precision=None):
    return lax.dot_general(
        a, b, (((1,), (1,)), ((), ())), preferred_element_type=F32, precision=precision
    )


def operands_kernel(
    stiff_hbm, rows_hbm, cols_hbm, count_hbm, probe_hbm, diag_hbm, off_hbm,
    weight_ref, basis_ref, level_ref, matrix_ref,
    got, stiff_ref, rows_ref, cols_ref, count_ref, key_ref, probe_ref, diag_ref, off_ref, wide, sums,
    send_sem, recv_sem, local_sem,
):
    sizes = [lax.axis_size(a) for a in ("gx", "gy", "gz")]
    here = [lax.axis_index(a) for a in ("gx", "gy", "gz")]
    slots, tiles = off_ref.shape[0], diag_ref.shape[0]
    faces = []
    for dim, size in enumerate(sizes):
        for step in (-1, 1):
            there = list(here)
            there[dim] = lax.rem(here[dim] + step + size, size)
            faces.append(tuple(there))
    barrier = pltpu.get_barrier_semaphore()
    for there in faces:
        pl.semaphore_signal(barrier, inc=1, device_id=there, device_id_type=MESH)
    loads = []
    for source, target in (
        (rows_hbm, rows_ref),
        (cols_hbm, cols_ref),
        (count_hbm, count_ref),
        (off_hbm, off_ref),
        (diag_hbm, diag_ref),
        (probe_hbm, probe_ref),
        (stiff_hbm, stiff_ref),
    ):
        load = pltpu.make_async_copy(source, target, local_sem.at[len(loads)])
        load.start()
        loads.append(load)
    pl.semaphore_wait(barrier, len(faces))
    copies = []
    for face, there in enumerate(faces):
        copy = pltpu.make_async_remote_copy(
            src_ref=stiff_hbm,
            dst_ref=got.at[face ^ 1],
            send_sem=send_sem.at[face],
            recv_sem=recv_sem.at[face ^ 1],
            device_id=there,
            device_id_type=MESH,
        )
        copy.start()
        copies.append(copy)

    for load in loads[:3]:
        load.wait()
    count = count_ref[0]
    for m in range(slots):
        key_ref[m] = jnp.where(m < count, rows_ref[m] * tiles + cols_ref[m], -1 - m)
    sums[slots] = jnp.zeros((TILE, TILE), F32)
    loads[3].wait()

    def add_tile(m, carry):
        key, before = key_ref[m], slots
        for other in range(slots - 1):
            before = jnp.where((other < m) & (key_ref[other] == key), other, before)
        sums[m] = off_ref[m].astype(F32) + sums[before]
        return carry

    lax.fori_loop(0, slots, add_tile, 0)

    def dense_block(place):
        last = slots
        for m in range(slots):
            last = jnp.where(key_ref[m] == place, m, last)
        return sums[last]

    for t in range(tiles):

        def put(u, carry, t=t):
            rows = pl.ds(pl.multiple_of(u * TILE, TILE), TILE)
            matrix_ref[rows, t * TILE : (t + 1) * TILE] = dense_block(t * tiles + u).T.astype(BF16)
            return carry

        lax.fori_loop(0, tiles, put, 0)
    loads[4].wait()
    eye = iota((TILE, TILE), 0) == iota((TILE, TILE), 1)
    for t in range(tiles):
        block = dense_block(t * tiles + t) + diag_ref[t].astype(F32)
        here_rows = slice(t * TILE, (t + 1) * TILE)
        level_ref[:, here_rows] = jnp.sum(jnp.where(eye, block, 0.0), axis=0, keepdims=True)
        matrix_ref[here_rows, here_rows] = jnp.where(eye, 0.0, block).T.astype(BF16)

    loads[5].wait()
    wide[...] = probe_ref[...].astype(F32)
    for t in range(tiles):
        basis_ref[:, t * TILE : (t + 1) * TILE] = wide[pl.ds(t, basis_ref.shape[0], stride=tiles), :]

    loads[6].wait()
    for copy in copies:
        copy.wait()
    zero = jnp.zeros(stiff_ref.shape, F32)
    stiff = stiff_ref[...]

    def face_value(face):
        dim, high = face // 2, face % 2
        inside = here[dim] < sizes[dim] - 1 if high else here[dim] > 0
        return jnp.where(inside, got[face], zero)

    total = face_value(1) + face_value(0)
    row = iota(stiff.shape, 0)
    y_low, y_high = face_value(2), face_value(3)
    total = total + jnp.where(row == 0, pltpu.roll(stiff, 1, 0), y_high[0:1, :])
    total = total + jnp.where(row == 1, pltpu.roll(stiff, 1, 0), y_low[1:2, :])
    lane = iota(stiff.shape, 1)
    z_low, z_high = face_value(4), face_value(5)
    width = stiff.shape[1]
    total = total + jnp.where(
        lane == width - 1, z_high[:, 0:1], pltpu.roll(stiff, width - 1, 1)
    )
    total = total + jnp.where(lane == 0, z_low[:, width - 1 : width], pltpu.roll(stiff, 1, 1))
    weight_ref[...] = stiff / (stiff + total / 6.0)


def in_hbm(x):
    return pltpu.with_memory_space_constraint(x, pltpu.HBM)


def sketch_operands(probes, stiff, diagonal, off_block, rows, cols, count):
    vmem = pl.BlockSpec(memory_space=pltpu.VMEM)
    hbm = pl.BlockSpec(memory_space=pltpu.HBM)
    dma = pltpu.SemaphoreType.DMA
    tiles, slots = diagonal.shape[0], off_block.shape[0]
    total = tiles * TILE
    return pl.pallas_call(
        operands_kernel,
        out_shape=(
            jax.ShapeDtypeStruct(stiff.shape, F32),
            jax.ShapeDtypeStruct((probes.shape[0] // tiles, total), F32),
            jax.ShapeDtypeStruct((1, total), F32),
            jax.ShapeDtypeStruct((total, total), BF16),
        ),
        in_specs=[hbm] * 7,
        out_specs=(vmem, vmem, vmem, vmem),
        scratch_shapes=[
            pltpu.VMEM((6,) + stiff.shape, F32),
            pltpu.VMEM(stiff.shape, F32),
            pltpu.SMEM(rows.shape, jnp.int32),
            pltpu.SMEM(cols.shape, jnp.int32),
            pltpu.SMEM(count.shape, jnp.int32),
            pltpu.SMEM(rows.shape, jnp.int32),
            pltpu.VMEM(probes.shape, BF16),
            pltpu.VMEM(diagonal.shape, BF16),
            pltpu.VMEM(off_block.shape, BF16),
            pltpu.VMEM(probes.shape, F32),
            pltpu.VMEM((slots + 1, TILE, TILE), F32),
            dma((6,)),
            dma((6,)),
            dma((7,)),
        ],
        compiler_params=pltpu.CompilerParams(
            collective_id=0, has_side_effects=True, vmem_limit_bytes=24 * 2**20
        ),
        name="sketch_operands",
    )(*map(in_hbm, (stiff, rows, cols)), count, *map(in_hbm, (probes, diagonal, off_block)))


def eliminate(gram):
    count = gram.shape[0]
    start = jnp.concatenate([gram, (iota(gram.shape, 0) == iota(gram.shape, 1)).astype(F32)], 1)
    row = iota((count, 1), 0)
    work = start
    pivots = jnp.zeros((count, 1), F32)
    for j in range(count):
        column = work[:, j : j + 1]
        pivot = column[j : j + 1, :]
        factor = jnp.where(row > j, column * (1.0 / pivot), 0.0)
        pivots = jnp.where(row == j, column, pivots)
        work = work - factor * work[j : j + 1, :]
    inverse = work[:, count:] * lax.rsqrt(pivots)
    original = jnp.sum(
        jnp.where(iota(gram.shape, 0) == iota(gram.shape, 1), gram, 0.0), axis=1, keepdims=True
    )
    return inverse, jnp.min(pivots / original)


def split(x):
    high = x.astype(BF16)
    return high, (x - high.astype(F32)).astype(BF16)


def basis_kernel(basis_ref, weight_ref, level_ref, matrix, defl_ref, field_ref, self_ref, wide):
    total = basis_ref.shape[1]
    tiles = total // TILE
    level = level_ref[...]
    weight = weight_ref[...]
    weight = jnp.concatenate([weight[0:1, :], weight[1:2, :]] * (tiles // 2), axis=1)
    step_weight = weight * (1.0 / SHIFT)

    def apply(high, low):
        both = jnp.dot(
            jnp.concatenate([high, low], axis=0), matrix[...], preferred_element_type=F32
        )
        return both[: high.shape[0]] + both[high.shape[0] :]

    def image_of(basis):
        scaled = basis * weight
        return basis - step_weight * (apply(*split(scaled)) + level * scaled)

    def normaliser(image):
        return eliminate(dot_nt(image, image, HIGHEST) * (1.0 / total))

    def finish(inverse, image):
        kept = jnp.dot(inverse, image, preferred_element_type=F32, precision=HIGHEST)[:DEFL]
        for t in range(tiles):
            wide[pl.ds(t, DEFL, stride=tiles), :] = kept[:, t * TILE : (t + 1) * TILE]
        defl_ref[...] = wide[...].astype(BF16)
        weighted = (kept * weight).astype(BF16)
        for t in range(tiles):
            field_ref[t % 2, :, t // 2 * TILE : (t // 2 + 1) * TILE] = weighted[
                :, t * TILE : (t + 1) * TILE
            ]
        applied = jnp.dot(weighted, matrix[...], preferred_element_type=F32)
        applied = applied + level * weighted.astype(F32)
        high, low = split(applied)
        self_ref[...] = (dot_nt(weighted, high) + dot_nt(weighted, low)) * (1.0 / total)

    image = basis_ref[...]
    for _ in range(ITERS):
        image = image_of(image)
    inverse, least = normaliser(image)
    finish(inverse, image)

    @pl.when(jnp.logical_not(least > SAFE_PIVOT))
    def _():
        def iteration(_, basis):
            image = image_of(basis)
            inverse, _ = normaliser(image)
            return jnp.dot(inverse, image, preferred_element_type=F32, precision=HIGHEST)

        basis = lax.fori_loop(0, ITERS - 1, iteration, basis_ref[...])
        image = image_of(basis)
        inverse, _ = normaliser(image)
        finish(inverse, image)


def local_basis(basis, weight, level, matrix):
    total = basis.shape[1]
    vmem = pl.BlockSpec(memory_space=pltpu.VMEM)
    return pl.pallas_call(
        basis_kernel,
        out_shape=(
            jax.ShapeDtypeStruct((DEFL * total // TILE, TILE), BF16),
            jax.ShapeDtypeStruct((2, DEFL, total // 2), BF16),
            jax.ShapeDtypeStruct((DEFL, DEFL), F32),
        ),
        in_specs=[vmem] * 4,
        out_specs=(vmem, vmem, vmem),
        scratch_shapes=[pltpu.VMEM((DEFL * total // TILE, TILE), F32)],
        compiler_params=pltpu.CompilerParams(vmem_limit_bytes=24 * 2**20),
        name="local_basis",
    )(basis, weight, level, matrix)


PLANE = 9
OWN = 4
PARTS = 16
PAYLOAD_ROWS = 16
ROW_GROUPS = 24
PAYLOAD_LANES = ROW_GROUPS * DEFL
BLOCK_GROUPS = PLANE * DEFL
END_GROUPS = 36


def plane_step(m):
    return m // 3 - 1, m % 3 - 1


def facing(m):
    return {-1: (1,), 0: (0, 1), 1: (0,)}[plane_step(m)[1]]


def end_group(m, y, c):
    before = sum(3 * len(facing(i)) for i in range(m))
    return before + 3 * facing(m).index(y) + c


def end_picker(y, half):
    row, lane = iota((PARTS, half), 0), iota((PARTS, half), 1)
    end, part = row // 8, row % 8
    hit = (part // 3 == y) & (part < 6) & (lane == (part % 3) * TILE + end * (TILE - 1))
    return hit.astype(BF16)


def payload_group(rows):
    group = DEFL + PARTS
    m, r = rows // group, rows % group
    first = jnp.zeros(rows.shape, jnp.int32)
    for i in range(1, PLANE):
        first = jnp.where(m == i, end_group(i, facing(i)[0], 0), first)
    low_y = jnp.where(m % 3 == 0, 1, 0)
    count = jnp.where(m % 3 == 1, 6, 3)
    end, part = (r - DEFL) // 8, (r - DEFL) % 8 - 3 * low_y
    used = (part >= 0) & (part < count)
    ends = jnp.where(used, BLOCK_GROUPS + end * END_GROUPS + first + part, -1)
    return jnp.where(r < DEFL, m * DEFL + r, ends)


def line_tree():
    side = [(0, 5), (0, 2), (2, 1), (2, 3), (5, 4), (5, 6), (5, 7)]
    return side + [(-a, -b) for a, b in side] + [(5, 8)]


def exchange_kernel(
    field_ref, self_ref, out_ref, full, sides, line_slots, send_sem, recv_sem, line_send, line_recv
):
    n_x, n_y, n_z = (lax.axis_size(a) for a in ("gx", "gy", "gz"))
    my_x, my_y, my_z = (lax.axis_index(a) for a in ("gx", "gy", "gz"))
    half = field_ref.shape[2]
    tree = line_tree()

    def device(m):
        step_x, step_y = plane_step(m)
        return (lax.rem(my_x + step_x + n_x, n_x), lax.rem(my_y + step_y + n_y, n_y), my_z)

    def line(step):
        return (my_x, my_y, lax.rem(my_z + step + n_z, n_z))

    neighbours = [m for m in range(PLANE) if m != OWN]
    distances = sorted({abs(b - a) for a, b in tree})
    barrier = pltpu.get_barrier_semaphore()
    for distance in reversed(distances):
        for step in (-distance, distance):
            pl.semaphore_signal(barrier, inc=1, device_id=line(step), device_id_type=MESH)
    for m in neighbours:
        pl.semaphore_signal(barrier, inc=1, device_id=device(m), device_id_type=MESH)
    pl.semaphore_wait(barrier, len(neighbours) + 2 * len(distances))

    slot = {m: i for i, m in enumerate(m for m in neighbours if plane_step(m)[1] != 0)}
    copies = []
    for m in neighbours:
        step_x, step_y = plane_step(m)
        back = PLANE - 1 - m
        if step_y == 0:
            source, target = field_ref, full.at[back // 3 // 2]
        else:
            source, target = field_ref.at[1 if step_y > 0 else 0], sides.at[slot[back]]
        copy = pltpu.make_async_remote_copy(
            src_ref=source,
            dst_ref=target,
            send_sem=send_sem.at[m],
            recv_sem=recv_sem.at[back],
            device_id=device(m),
            device_id_type=MESH,
        )
        copy.start()
        copies.append(copy)

    pick = [end_picker(y, half) for y in range(2)]
    own = [field_ref[y] for y in range(2)]
    stack = [[jnp.concatenate([-own[y], pick[z]], axis=0) for z in range(2)] for y in range(2)]
    lanes = PAYLOAD_LANES
    spread = (iota((DEFL, lanes), 1) % DEFL == iota((DEFL, lanes), 0)).astype(BF16)
    rows = PLANE * (DEFL + PARTS)
    place = payload_group(iota((rows, 1), 0)) % ROW_GROUPS
    keep = iota((rows, lanes), 1) // DEFL == place
    target = payload_group(iota((PAYLOAD_ROWS, rows), 1))
    gather = (target >= 0) & (target // ROW_GROUPS == iota((PAYLOAD_ROWS, rows), 0))
    gather = gather.astype(BF16)
    for copy in copies:
        copy.wait_recv()

    parts = []
    for m in range(PLANE):
        step_x, step_y = plane_step(m)
        if m == OWN:
            ends = dot_nt(pick[0], own[0]) + dot_nt(pick[1], own[1])
            parts.append(jnp.concatenate([self_ref[...], ends], axis=0))
            continue
        if step_y == 0:
            side = m // 3 // 2
            block = dot_nt(stack[0][0], full[side, 0]) + dot_nt(stack[1][1], full[side, 1])
        elif step_y < 0:
            block = dot_nt(stack[0][1], sides[slot[m]])
        else:
            block = dot_nt(stack[1][0], sides[slot[m]])
        inside = True
        if step_x != 0:
            inside = my_x < n_x - 1 if step_x > 0 else my_x > 0
        if step_y != 0:
            inside = jnp.logical_and(inside, my_y < n_y - 1 if step_y > 0 else my_y > 0)
        parts.append(jnp.where(inside, block, 0.0))
    parts = jnp.concatenate(parts, axis=0).astype(BF16)

    wide = jnp.dot(parts, spread, preferred_element_type=F32)
    wide = jnp.where(keep, wide, 0.0).astype(BF16)
    line_slots[my_z] = jnp.dot(gather, wide, preferred_element_type=F32).astype(BF16)

    sign = 1 - 2 * lax.rem(my_x, 2)
    hops = {}

    def send(parent, child):
        owner = line_slots.at[lax.rem(my_z - sign * parent + n_z, n_z)]
        hop = pltpu.make_async_remote_copy(
            src_ref=owner,
            dst_ref=owner,
            send_sem=line_send.at[child + n_z // 2],
            recv_sem=line_recv.at[child + n_z // 2],
            device_id=line(sign * (child - parent)),
            device_id_type=MESH,
        )
        hop.start()
        hops[child] = hop

    for parent, child in tree:
        if parent == 0:
            send(parent, child)
    parents = [p for p in sorted({p for p, _ in tree}, key=abs) if p != 0]
    for p in parents:
        hops[p].wait_recv()
        for parent, child in tree:
            if parent == p:
                send(parent, child)
    for child, hop in hops.items():
        if child not in parents:
            hop.wait_recv()
    for copy in copies + list(hops.values()):
        copy.wait_send()
    out_ref[...] = line_slots[...]


def exchange(field, self_block, n_z):
    vmem = pl.BlockSpec(memory_space=pltpu.VMEM)
    dma = pltpu.SemaphoreType.DMA
    half = field.shape[2]
    payload = (n_z, PAYLOAD_ROWS, PAYLOAD_LANES)
    return pl.pallas_call(
        exchange_kernel,
        out_shape=jax.ShapeDtypeStruct(payload, BF16),
        in_specs=[vmem, vmem],
        out_specs=vmem,
        scratch_shapes=[
            pltpu.VMEM((2, 2, DEFL, half), BF16),
            pltpu.VMEM((6, DEFL, half), BF16),
            pltpu.VMEM(payload, BF16),
            dma((PLANE,)),
            dma((PLANE,)),
            dma((n_z + 1,)),
            dma((n_z + 1,)),
        ],
        compiler_params=pltpu.CompilerParams(
            collective_id=1, has_side_effects=True, vmem_limit_bytes=24 * 2**20
        ),
        name="exchange",
    )(field, self_block)


def pair_index(m, step_z):
    flat = 3 * m + step_z + 1
    return flat if flat < 13 else flat - 1


def unpack_kernel(gathered_ref, self_ref, pairs_ref):
    n_z = self_ref.shape[0]
    width = DEFL * DEFL
    packed = gathered_ref[...]
    column = iota((1, n_z * PAYLOAD_ROWS), 1)

    def select(first, count, shift):
        index = iota((count * n_z, 1), 0)
        member = index % n_z + shift
        inside = (member >= 0) & (member < n_z)
        wanted = jnp.where(inside, member * PAYLOAD_ROWS + first + index // n_z, -1)
        hit = (column == wanted).astype(BF16)
        return jnp.dot(hit, packed, preferred_element_type=F32)

    block_rows = BLOCK_GROUPS // ROW_GROUPS
    rows = select(0, block_rows, 0)
    for m in range(PLANE):
        pieces, group = [], m * DEFL
        while group < (m + 1) * DEFL:
            row, start = group // ROW_GROUPS, group % ROW_GROUPS
            stop = min(ROW_GROUPS, start + (m + 1) * DEFL - group)
            pieces.append(rows[row * n_z : (row + 1) * n_z, start * DEFL : stop * DEFL])
            group += stop - start
        block = jnp.concatenate(pieces, axis=1)
        if m == OWN:
            self_ref[...] = block
        else:
            pairs_ref[pair_index(m, 0)] = block

    per_tile = TILE // DEFL
    row_tiles = ROW_GROUPS // per_tile
    end_tiles = END_GROUPS // per_tile
    end_rows = 2 * END_GROUPS // ROW_GROUPS

    def tile_of(rows, number):
        row, i = number // row_tiles, number % row_tiles
        return rows[row * n_z : (row + 1) * n_z, i * TILE : (i + 1) * TILE]

    own_first = end_group(OWN, 0, 0) // per_tile
    own_count = end_group(OWN, 1, 2) // per_tile + 1 - own_first
    rows = select(block_rows, end_rows, 0).astype(BF16)
    own_tiles = jnp.concatenate(
        [tile_of(rows, end * end_tiles + own_first + i) for end in range(2) for i in range(own_count)],
        axis=0,
    )
    value, lane = iota((TILE, width), 0), iota((TILE, width), 1)
    own = []
    for v in range(per_tile):
        spread = jnp.where(value == v * DEFL + lane // DEFL, -1.0, 0.0).astype(BF16)
        own.append(jnp.dot(own_tiles, spread, preferred_element_type=F32))

    def own_part(end, y, c):
        group = end_group(OWN, y, c)
        start = (end * own_count + group // per_tile - own_first) * n_z
        return own[group % per_tile][start : start + n_z]

    value, lane = iota((TILE, per_tile * TILE), 0), iota((TILE, per_tile * TILE), 1)
    repeat = (value == lane // TILE * DEFL + lane % DEFL).astype(BF16)
    for step_z in (-1, 1):
        their_end, own_end = (0, 1) if step_z > 0 else (1, 0)
        rows = select(block_rows, end_rows, step_z).astype(BF16)
        tiles = [tile_of(rows, their_end * end_tiles + i) for i in range(end_tiles)]
        theirs = jnp.dot(jnp.concatenate(tiles, axis=0), repeat, preferred_element_type=F32)
        for m in range(PLANE):
            step_y = plane_step(m)[1]
            pairs = [(0, 0), (1, 1)] if step_y == 0 else [(0, 1)] if step_y < 0 else [(1, 0)]
            total = None
            for own_y, their_y in pairs:
                for c in range(3):
                    group = end_group(m, their_y, c)
                    start, v = group // per_tile * n_z, group % per_tile
                    right = theirs[start : start + n_z, v * TILE : (v + 1) * TILE]
                    right = jnp.concatenate([right] * (width // TILE), axis=1)
                    term = own_part(own_end, own_y, c) * right
                    total = term if total is None else total + term
            pairs_ref[pair_index(m, step_z)] = total


def unpack(gathered, n_z):
    vmem = pl.BlockSpec(memory_space=pltpu.VMEM)
    width = DEFL * DEFL
    return pl.pallas_call(
        unpack_kernel,
        out_shape=(
            jax.ShapeDtypeStruct((n_z, width), F32),
            jax.ShapeDtypeStruct((26, n_z, width), F32),
        ),
        in_specs=[vmem],
        out_specs=(vmem, vmem),
        compiler_params=pltpu.CompilerParams(vmem_limit_bytes=32 * 2**20),
        name="unpack",
    )(gathered.reshape(n_z * PAYLOAD_ROWS, PAYLOAD_LANES))


def per_device(probes, stiffness, diag_tiles, off_tiles, off_rows, off_cols, off_count):
    n_z = lax.axis_size("gz")
    cell_shape = probes.shape[1:]
    weight, basis, level, matrix = sketch_operands(
        probes.reshape(-1, TILE),
        stiffness[0],
        diag_tiles[0, 0, 0],
        off_tiles[0, 0, 0],
        off_rows[0, 0, 0],
        off_cols[0, 0, 0],
        off_count[0, 0],
    )
    deflation, field, self_block = local_basis(basis, weight, level, matrix)
    gathered = exchange(field, self_block, n_z)
    coarse_self, coarse_pairs = unpack(gathered, n_z)
    return (
        deflation.reshape((DEFL,) + cell_shape),
        coarse_self[None, None],
        coarse_pairs.transpose(1, 0, 2)[None, None],
    )


def solution(mesh):
    placed = (
        P(None, None, "gx", "gy", "gz"),
        P("gx", "gy", "gz"),
        P("gx", "gy", "gz", None, None, None),
        P("gx", "gy", "gz", None, None, None),
        P("gx", "gy", "gz", None),
        P("gx", "gy", "gz", None),
        P("gx", "gy", "gz"),
    )
    return jax.shard_map(
        per_device,
        mesh=mesh,
        in_specs=placed,
        out_specs=(
            P(None, None, "gx", "gy", "gz"),
            P("gx", "gy", None, None),
            P("gx", "gy", None, None, None),
        ),
        check_vma=False,
    )
```

time: 72.7 us -> 53.4 us (0.73)
  the two profiles are of different devices: /device:TPU:8 before, /device:TPU:1 now
where the time goes in v1:
time: 53.4 us; the launch traced here: 52.4 us
  Pallas kernels  51.1 us (96%)
  between operations  1.3 us (2%)
    pallas_call x1, Pallas kernels, exchange(): pl.pallas_call(exchange_kernel, out_shape=jax.ShapeDtypeStruct(payload, B...  23.2 us
    pallas_call x1, Pallas kernels, sketch_operands(): pl.pallas_call(operands_kernel, out_shape=(jax.ShapeDtypeStruct(stiff.sha...  16.6 us
    pallas_call x1, Pallas kernels, local_basis(): pl.pallas_call(basis_kernel, out_shape=(jax.ShapeDtypeStruct((DEFL * tota...  8.96 us
    pallas_call x1, Pallas kernels, unpack(): pl.pallas_call(unpack_kernel, out_shape=(jax.ShapeDtypeStruct((n_z, width...  2.36 us

profile of v1, /device:TPU:1, one launch (start us, length us, event | category | flops | bytes accessed | tf_op | source)
XLA Modules:
  0.0 52.4 jit_solution(907953948890504156)
XLA Ops:
  1.3 16.6 %sketch_operands.1 = (f32[2,128]{1,0:T(2,128)S(1)}, f32[48,768]{1,0:T(8,128)S(1)}, f32[1,768]{1,0:T(1,128)S(1)}, bf16[768,768]{1,0:T(8,128)(2,1)S(1)}) custom-call(f32[2,128]{1,0:T(2,128)} %bitcast.20, s32[24]{0:T(128)} %bitcast.21, s32[24]{0:T(128)} %bitcast.22, s32[1]{0:T(128)} %bitcast.15.count_hbm, bf16[288,128]{1,0:T(8,128)(2,1)} %bitcast.19, ...), custom_call_target="tpu_custom_call" | custom-call | tf_op jit(solution)/shard_map/sketch_operands/pallas_call | solution.py:155
  17.9 9.0 %local_basis.1 = (bf16[192,128]{1,0:T(8,128)(2,1)}, bf16[2,32,384]{2,1,0:T(8,128)(2,1)S(1)}, f32[32,32]{1,0:T(8,128)S(1)}) custom-call(f32[48,768]{1,0:T(8,128)S(1)} %get-tuple-element.12.basis_ref, f32[2,128]{1,0:T(2,128)S(1)} %get-tuple-element.13.weight_ref, f32[1,768]{1,0:T(1,128)S(1)} %get-tuple-element.14.level_ref, ...), custom_call_target="tpu_custom_call" | custom-call | tf_op jit(solution)/shard_map/local_basis/pallas_call | solution.py:270
  26.9 23.2 %exchange.1 = bf16[16,16,768]{2,1,0:T(8,128)(2,1)S(1)} custom-call(bf16[2,32,384]{2,1,0:T(8,128)(2,1)S(1)} %get-tuple-element.17.field_ref, f32[32,32]{1,0:T(8,128)S(1)} %get-tuple-element.18.self_ref), custom_call_target="tpu_custom_call" | custom-call | tf_op jit(solution)/shard_map/exchange/pallas_call | solution.py:457
  50.0 2.4 %unpack.1 = (f32[16,1024]{1,0:T(8,128)}, f32[26,16,1024]{2,1,0:T(8,128)}) custom-call(bf16[256,768]{1,0:T(8,128)(2,1)S(1)} %bitcast.16), custom_call_target="tpu_custom_call" | custom-call | tf_op jit(solution)/shard_map/unpack/pallas_call | solution.py:564

commit v2 on v1

--- a/solution.py
+++ b/solution.py
@@ -15,6 +15,7 @@
 SHIFT = 8.0
 TILE = 128
 SAFE_PIVOT = 0.01
+PANEL = 8
 
 
 def iota(shape, dim):
@@ -95,21 +96,17 @@
             last = jnp.where(key_ref[m] == place, m, last)
         return sums[last]
 
-    for t in range(tiles):
-
-        def put(u, carry, t=t):
-            rows = pl.ds(pl.multiple_of(u * TILE, TILE), TILE)
-            matrix_ref[rows, t * TILE : (t + 1) * TILE] = dense_block(t * tiles + u).T.astype(BF16)
-            return carry
-
-        lax.fori_loop(0, tiles, put, 0)
     loads[4].wait()
     eye = iota((TILE, TILE), 0) == iota((TILE, TILE), 1)
     for t in range(tiles):
-        block = dense_block(t * tiles + t) + diag_ref[t].astype(F32)
-        here_rows = slice(t * TILE, (t + 1) * TILE)
-        level_ref[:, here_rows] = jnp.sum(jnp.where(eye, block, 0.0), axis=0, keepdims=True)
-        matrix_ref[here_rows, here_rows] = jnp.where(eye, 0.0, block).T.astype(BF16)
+        columns = slice(t * TILE, (t + 1) * TILE)
+        for u in range(tiles):
+            block = dense_block(t * tiles + u)
+            if t == u:
+                block = block + diag_ref[t].astype(F32)
+                level_ref[:, columns] = jnp.sum(jnp.where(eye, block, 0.0), axis=0, keepdims=True)
+                block = jnp.where(eye, 0.0, block)
+            matrix_ref[u * TILE : (u + 1) * TILE, columns] = block.astype(BF16).T
 
     loads[5].wait()
     wide[...] = probe_ref[...].astype(F32)
@@ -188,15 +185,23 @@
 def eliminate(gram):
     count = gram.shape[0]
     start = jnp.concatenate([gram, (iota(gram.shape, 0) == iota(gram.shape, 1)).astype(F32)], 1)
-    row = iota((count, 1), 0)
+    rows_done, pivots_done = [], []
     work = start
-    pivots = jnp.zeros((count, 1), F32)
-    for j in range(count):
-        column = work[:, j : j + 1]
-        pivot = column[j : j + 1, :]
-        factor = jnp.where(row > j, column * (1.0 / pivot), 0.0)
-        pivots = jnp.where(row == j, column, pivots)
-        work = work - factor * work[j : j + 1, :]
+    for first in range(0, count, PANEL):
+        row = iota((count - first, 1), 0)
+        columns = [
+            jnp.broadcast_to(work[:, j : j + 1], work.shape) for j in range(first, first + PANEL)
+        ]
+        for i in range(PANEL):
+            factor = jnp.where(row > i, columns[i] * (1.0 / columns[i][i : i + 1, :]), 0.0)
+            pivots_done.append(columns[i][i : i + 1, :count])
+            for k in range(i + 1, PANEL):
+                columns[k] = columns[k] - factor * columns[k][i : i + 1, :]
+            work = work - factor * work[i : i + 1, :]
+        rows_done.append(work[:PANEL])
+        work = work[PANEL:]
+    work = jnp.concatenate(rows_done, axis=0)
+    pivots = jnp.concatenate(pivots_done, axis=0)[:, :1]
     inverse = work[:, count:] * lax.rsqrt(pivots)
     original = jnp.sum(
         jnp.where(iota(gram.shape, 0) == iota(gram.shape, 1), gram, 0.0), axis=1, keepdims=True
@@ -209,47 +214,34 @@
     return high, (x - high.astype(F32)).astype(BF16)
 
 
-def basis_kernel(basis_ref, weight_ref, level_ref, matrix, defl_ref, field_ref, self_ref, wide):
+def unknown_weights(weight, tiles):
+    return jnp.concatenate([weight[0:1, :], weight[1:2, :]] * (tiles // 2), axis=1)
+
+
+def image_kernel(basis_ref, weight_ref, level_ref, matrix, inverse_ref, image_ref):
     total = basis_ref.shape[1]
-    tiles = total // TILE
     level = level_ref[...]
-    weight = weight_ref[...]
-    weight = jnp.concatenate([weight[0:1, :], weight[1:2, :]] * (tiles // 2), axis=1)
+    weight = unknown_weights(weight_ref[...], total // TILE)
     step_weight = weight * (1.0 / SHIFT)
 
-    def apply(high, low):
+    def image_of(basis):
+        scaled = basis * weight
+        high, low = split(scaled)
         both = jnp.dot(
             jnp.concatenate([high, low], axis=0), matrix[...], preferred_element_type=F32
         )
-        return both[: high.shape[0]] + both[high.shape[0] :]
-
-    def image_of(basis):
-        scaled = basis * weight
-        return basis - step_weight * (apply(*split(scaled)) + level * scaled)
+        applied = both[: high.shape[0]] + both[high.shape[0] :] + level * scaled
+        return basis - step_weight * applied
 
     def normaliser(image):
         return eliminate(dot_nt(image, image, HIGHEST) * (1.0 / total))
-
-    def finish(inverse, image):
-        kept = jnp.dot(inverse, image, preferred_element_type=F32, precision=HIGHEST)[:DEFL]
-        for t in range(tiles):
-            wide[pl.ds(t, DEFL, stride=tiles), :] = kept[:, t * TILE : (t + 1) * TILE]
-        defl_ref[...] = wide[...].astype(BF16)
-        weighted = (kept * weight).astype(BF16)
-        for t in range(tiles):
-            field_ref[t % 2, :, t // 2 * TILE : (t // 2 + 1) * TILE] = weighted[
-                :, t * TILE : (t + 1) * TILE
-            ]
-        applied = jnp.dot(weighted, matrix[...], preferred_element_type=F32)
-        applied = applied + level * weighted.astype(F32)
-        high, low = split(applied)
-        self_ref[...] = (dot_nt(weighted, high) + dot_nt(weighted, low)) * (1.0 / total)
 
     image = basis_ref[...]
     for _ in range(ITERS):
         image = image_of(image)
     inverse, least = normaliser(image)
-    finish(inverse, image)
+    inverse_ref[...] = inverse
+    image_ref[...] = image
 
     @pl.when(jnp.logical_not(least > SAFE_PIVOT))
     def _():
@@ -261,24 +253,23 @@
         basis = lax.fori_loop(0, ITERS - 1, iteration, basis_ref[...])
         image = image_of(basis)
         inverse, _ = normaliser(image)
-        finish(inverse, image)
-
-
-def local_basis(basis, weight, level, matrix):
-    total = basis.shape[1]
+        inverse_ref[...] = inverse
+        image_ref[...] = image
+
+
+def last_image(basis, weight, level, matrix):
+    probes = basis.shape[0]
     vmem = pl.BlockSpec(memory_space=pltpu.VMEM)
     return pl.pallas_call(
-        basis_kernel,
+        image_kernel,
         out_shape=(
-            jax.ShapeDtypeStruct((DEFL * total // TILE, TILE), BF16),
-            jax.ShapeDtypeStruct((2, DEFL, total // 2), BF16),
-            jax.ShapeDtypeStruct((DEFL, DEFL), F32),
+            jax.ShapeDtypeStruct((probes, probes), F32),
+            jax.ShapeDtypeStruct(basis.shape, F32),
         ),
         in_specs=[vmem] * 4,
-        out_specs=(vmem, vmem, vmem),
-        scratch_shapes=[pltpu.VMEM((DEFL * total // TILE, TILE), F32)],
+        out_specs=(vmem, vmem),
         compiler_params=pltpu.CompilerParams(vmem_limit_bytes=24 * 2**20),
-        name="local_basis",
+        name="last_image",
     )(basis, weight, level, matrix)
 
 
@@ -332,7 +323,9 @@
 
 
 def exchange_kernel(
-    field_ref, self_ref, out_ref, full, sides, line_slots, send_sem, recv_sem, line_send, line_recv
+    inverse_ref, image_ref, weight_ref, level_ref, matrix_ref,
+    out_ref, defl_ref,
+    field_ref, full, sides, line_slots, wide_ref, send_sem, recv_sem, line_send, line_recv,
 ):
     n_x, n_y, n_z = (lax.axis_size(a) for a in ("gx", "gy", "gz"))
     my_x, my_y, my_z = (lax.axis_index(a) for a in ("gx", "gy", "gz"))
@@ -354,6 +347,18 @@
             pl.semaphore_signal(barrier, inc=1, device_id=line(step), device_id_type=MESH)
     for m in neighbours:
         pl.semaphore_signal(barrier, inc=1, device_id=device(m), device_id_type=MESH)
+
+    total = image_ref.shape[1]
+    tiles = total // TILE
+    basis = jnp.dot(
+        inverse_ref[...], image_ref[...], preferred_element_type=F32, precision=HIGHEST
+    )
+    kept = basis[:DEFL]
+    weighted = (kept * unknown_weights(weight_ref[...], tiles)).astype(BF16)
+    for t in range(tiles):
+        field_ref[t % 2, :, t // 2 * TILE : (t // 2 + 1) * TILE] = weighted[
+            :, t * TILE : (t + 1) * TILE
+        ]
     pl.semaphore_wait(barrier, len(neighbours) + 2 * len(distances))
 
     slot = {m: i for i, m in enumerate(m for m in neighbours if plane_step(m)[1] != 0)}
@@ -376,6 +381,14 @@
         copy.start()
         copies.append(copy)
 
+    for t in range(tiles):
+        wide_ref[pl.ds(t, DEFL, stride=tiles), :] = kept[:, t * TILE : (t + 1) * TILE]
+    defl_ref[...] = wide_ref[...].astype(BF16)
+    applied = jnp.dot(weighted, matrix_ref[...], preferred_element_type=F32)
+    applied = applied + level_ref[...] * weighted.astype(F32)
+    high, low = split(applied)
+    self_block = (dot_nt(weighted, high) + dot_nt(weighted, low)) * (1.0 / total)
+
     pick = [end_picker(y, half) for y in range(2)]
     own = [field_ref[y] for y in range(2)]
     stack = [[jnp.concatenate([-own[y], pick[z]], axis=0) for z in range(2)] for y in range(2)]
@@ -395,7 +408,7 @@
         step_x, step_y = plane_step(m)
         if m == OWN:
             ends = dot_nt(pick[0], own[0]) + dot_nt(pick[1], own[1])
-            parts.append(jnp.concatenate([self_ref[...], ends], axis=0))
+            parts.append(jnp.concatenate([self_block, ends], axis=0))
             continue
         if step_y == 0:
             side = m // 3 // 2
@@ -449,20 +462,26 @@
     out_ref[...] = line_slots[...]
 
 
-def exchange(field, self_block, n_z):
+def exchange(inverse, image, weight, level, matrix, n_z):
     vmem = pl.BlockSpec(memory_space=pltpu.VMEM)
     dma = pltpu.SemaphoreType.DMA
-    half = field.shape[2]
+    total = image.shape[1]
     payload = (n_z, PAYLOAD_ROWS, PAYLOAD_LANES)
+    rows = DEFL * total // TILE
     return pl.pallas_call(
         exchange_kernel,
-        out_shape=jax.ShapeDtypeStruct(payload, BF16),
-        in_specs=[vmem, vmem],
-        out_specs=vmem,
+        out_shape=(
+            jax.ShapeDtypeStruct(payload, BF16),
+            jax.ShapeDtypeStruct((rows, TILE), BF16),
+        ),
+        in_specs=[vmem] * 5,
+        out_specs=(vmem, vmem),
         scratch_shapes=[
-            pltpu.VMEM((2, 2, DEFL, half), BF16),
-            pltpu.VMEM((6, DEFL, half), BF16),
+            pltpu.VMEM((2, DEFL, total // 2), BF16),
+            pltpu.VMEM((2, 2, DEFL, total // 2), BF16),
+            pltpu.VMEM((6, DEFL, total // 2), BF16),
             pltpu.VMEM(payload, BF16),
+            pltpu.VMEM((rows, TILE), F32),
             dma((PLANE,)),
             dma((PLANE,)),
             dma((n_z + 1,)),
@@ -472,7 +491,7 @@
             collective_id=1, has_side_effects=True, vmem_limit_bytes=24 * 2**20
         ),
         name="exchange",
-    )(field, self_block)
+    )(inverse, image, weight, level, matrix)
 
 
 def pair_index(m, step_z):
@@ -480,9 +499,23 @@
     return flat if flat < 13 else flat - 1
 
 
-def unpack_kernel(gathered_ref, self_ref, pairs_ref):
+def unpack_kernel(
+    gathered_ref, kept_ref, self_hbm, pairs_hbm, defl_hbm, self_ref, pairs_ref, sem
+):
     n_z = self_ref.shape[0]
     width = DEFL * DEFL
+    stores = []
+
+    def store(source, target):
+        copy = pltpu.make_async_copy(source, target, sem.at[len(stores)])
+        copy.start()
+        stores.append(copy)
+
+    def store_pair(index, block):
+        pairs_ref[index] = block
+        store(pairs_ref.at[index], pairs_hbm.at[index])
+
+    store(kept_ref, defl_hbm)
     packed = gathered_ref[...]
     column = iota((1, n_z * PAYLOAD_ROWS), 1)
 
@@ -506,8 +539,9 @@
         block = jnp.concatenate(pieces, axis=1)
         if m == OWN:
             self_ref[...] = block
+            store(self_ref, self_hbm)
         else:
-            pairs_ref[pair_index(m, 0)] = block
+            store_pair(pair_index(m, 0), block)
 
     per_tile = TILE // DEFL
     row_tiles = ROW_GROUPS // per_tile
@@ -555,23 +589,33 @@
                     right = jnp.concatenate([right] * (width // TILE), axis=1)
                     term = own_part(own_end, own_y, c) * right
                     total = term if total is None else total + term
-            pairs_ref[pair_index(m, step_z)] = total
-
-
-def unpack(gathered, n_z):
+            store_pair(pair_index(m, step_z), total)
+    for copy in stores:
+        copy.wait()
+
+
+def unpack(gathered, kept, n_z):
     vmem = pl.BlockSpec(memory_space=pltpu.VMEM)
+    hbm = pl.BlockSpec(memory_space=pltpu.HBM)
     width = DEFL * DEFL
+    pairs = 3 * PLANE - 1
     return pl.pallas_call(
         unpack_kernel,
         out_shape=(
             jax.ShapeDtypeStruct((n_z, width), F32),
-            jax.ShapeDtypeStruct((26, n_z, width), F32),
+            jax.ShapeDtypeStruct((pairs, n_z, width), F32),
+            jax.ShapeDtypeStruct(kept.shape, kept.dtype),
         ),
-        in_specs=[vmem],
-        out_specs=(vmem, vmem),
+        in_specs=[vmem, vmem],
+        out_specs=(hbm, hbm, hbm),
+        scratch_shapes=[
+            pltpu.VMEM((n_z, width), F32),
+            pltpu.VMEM((pairs, n_z, width), F32),
+            pltpu.SemaphoreType.DMA((pairs + 2,)),
+        ],
         compiler_params=pltpu.CompilerParams(vmem_limit_bytes=32 * 2**20),
         name="unpack",
-    )(gathered.reshape(n_z * PAYLOAD_ROWS, PAYLOAD_LANES))
+    )(gathered.reshape(n_z * PAYLOAD_ROWS, PAYLOAD_LANES), kept)
 
 
 def per_device(probes, stiffness, diag_tiles, off_tiles, off_rows, off_cols, off_count):
@@ -586,9 +630,9 @@
         off_cols[0, 0, 0],
         off_count[0, 0],
     )
-    deflation, field, self_block = local_basis(basis, weight, level, matrix)
-    gathered = exchange(field, self_block, n_z)
-    coarse_self, coarse_pairs = unpack(gathered, n_z)
+    inverse, image = last_image(basis, weight, level, matrix)
+    gathered, kept = exchange(inverse, image, weight, level, matrix, n_z)
+    coarse_self, coarse_pairs, deflation = unpack(gathered, kept, n_z)
     return (
         deflation.reshape((DEFL,) + cell_shape),
         coarse_self[None, None],

time: 53.4 us -> 47.9 us (0.90); the launches traced: 52.4 us -> 47.7 us
  Pallas kernels: 51.1 us -> 46.4 us
    pallas_call x2, Pallas kernels: 32.1 us -> 29.2 us  [the longest x1 24.5 us: exchange(): pl.pallas_call(exchange_kernel, out_shape=(jax.ShapeDtypeStruct(payload,...]
    pallas_call x1, Pallas kernels: 16.6 us -> 15.1 us  [sketch_operands(): pl.pallas_call(operands_kernel, out_shape=(jax.ShapeDtypeStruct(stiff.sha...]
where the time goes in v2:
time: 47.9 us; the launch traced here: 47.7 us
  Pallas kernels  46.4 us (97%)
  between operations  1.3 us (3%)
    pallas_call x1, Pallas kernels, exchange(): pl.pallas_call(exchange_kernel, out_shape=(jax.ShapeDtypeStruct(payload,...  24.5 us
    pallas_call x1, Pallas kernels, sketch_operands(): pl.pallas_call(operands_kernel, out_shape=(jax.ShapeDtypeStruct(stiff.sha...  15.1 us
    pallas_call x1, Pallas kernels, last_image(): pl.pallas_call(image_kernel, out_shape=(jax.ShapeDtypeStruct((probes, pro...  4.72 us
    pallas_call x1, Pallas kernels, unpack(): pl.pallas_call(unpack_kernel, out_shape=(jax.ShapeDtypeStruct((n_z, width...  2.12 us

profile of v2, /device:TPU:1, one launch (start us, length us, event | category | flops | bytes accessed | tf_op | source)
XLA Modules:
  0.0 47.7 jit_solution(2644355511784056709)
XLA Ops:
  1.3 15.1 %sketch_operands.1 = (f32[2,128]{1,0:T(2,128)S(1)}, f32[48,768]{1,0:T(8,128)S(1)}, f32[1,768]{1,0:T(1,128)S(1)}, bf16[768,768]{1,0:T(8,128)(2,1)S(1)}) custom-call(f32[2,128]{1,0:T(2,128)} %bitcast.20, s32[24]{0:T(128)} %bitcast.21, s32[24]{0:T(128)} %bitcast.22, s32[1]{0:T(128)} %bitcast.15.count_hbm, bf16[288,128]{1,0:T(8,128)(2,1)} %bitcast.19, ...), custom_call_target="tpu_custom_call" | custom-call | tf_op jit(solution)/shard_map/sketch_operands/pallas_call | solution.py:152
  16.4 4.7 %last_image.1 = (f32[48,48]{1,0:T(8,128)S(1)}, f32[48,768]{1,0:T(8,128)S(1)}) custom-call(f32[48,768]{1,0:T(8,128)S(1)} %get-tuple-element.14.basis_ref, f32[2,128]{1,0:T(2,128)S(1)} %get-tuple-element.15.weight_ref, f32[1,768]{1,0:T(1,128)S(1)} %get-tuple-element.16.level_ref, bf16[768,768]{1,0:T(8,128)(2,1)S(1)} %get-tuple-element.17.matrix.matrix_ref), custom_call_target="tpu_custom_call" | custom-call | tf_op jit(solution)/shard_map/last_image/pallas_call | solution.py:263
  21.1 24.5 %exchange.1 = (bf16[16,16,768]{2,1,0:T(8,128)(2,1)S(1)}, bf16[192,128]{1,0:T(8,128)(2,1)S(1)}) custom-call(f32[48,48]{1,0:T(8,128)S(1)} %get-tuple-element.18.inverse_ref, f32[48,768]{1,0:T(8,128)S(1)} %get-tuple-element.19.image_ref, f32[2,128]{1,0:T(2,128)S(1)} %get-tuple-element.15.weight_ref, f32[1,768]{1,0:T(1,128)S(1)} %get-tuple-element.16.level_ref, ...), custom_call_target="tpu_custom_call" | custom-call | tf_op jit(solution)/shard_map/exchange/pallas_call | solution.py:471
  45.6 2.1 %unpack.1 = (f32[16,1024]{1,0:T(8,128)}, f32[26,16,1024]{2,1,0:T(8,128)}, bf16[192,128]{1,0:T(8,128)(2,1)}) custom-call(bf16[256,768]{1,0:T(8,128)(2,1)S(1)} %bitcast.16, bf16[192,128]{1,0:T(8,128)(2,1)S(1)} %get-tuple-element.21.kept_ref), custom_call_target="tpu_custom_call" | custom-call | tf_op jit(solution)/shard_map/unpack/pallas_call | solution.py:602

commit v3 on v2

--- a/solution.py
+++ b/solution.py
@@ -1,3 +1,5 @@
+import functools
+
 import jax
 import jax.numpy as jnp
 from jax import lax
@@ -20,6 +22,14 @@
 
 def iota(shape, dim):
     return lax.broadcasted_iota(jnp.int32, shape, dim)
+
+
+def over(x, n):
+    return x >> (n.bit_length() - 1) if n & (n - 1) == 0 else x // n
+
+
+def modulo(x, n):
+    return x & (n - 1) if n & (n - 1) == 0 else x % n
 
 
 def dot_nt(a, b, precision=None):
@@ -194,19 +204,20 @@
         ]
         for i in range(PANEL):
             factor = jnp.where(row > i, columns[i] * (1.0 / columns[i][i : i + 1, :]), 0.0)
-            pivots_done.append(columns[i][i : i + 1, :count])
+            pivots_done.append(columns[i][i : i + 1, :])
             for k in range(i + 1, PANEL):
                 columns[k] = columns[k] - factor * columns[k][i : i + 1, :]
             work = work - factor * work[i : i + 1, :]
         rows_done.append(work[:PANEL])
         work = work[PANEL:]
     work = jnp.concatenate(rows_done, axis=0)
-    pivots = jnp.concatenate(pivots_done, axis=0)[:, :1]
-    inverse = work[:, count:] * lax.rsqrt(pivots)
+    pivots = jnp.concatenate(pivots_done, axis=0)
+    inverse = work[:, count:] * lax.rsqrt(pivots[:, :count])
     original = jnp.sum(
         jnp.where(iota(gram.shape, 0) == iota(gram.shape, 1), gram, 0.0), axis=1, keepdims=True
     )
-    return inverse, jnp.min(pivots / original)
+    safe = jnp.where(pivots > SAFE_PIVOT * original, 1.0, 0.0)
+    return inverse, jnp.min(safe, axis=0, keepdims=True)
 
 
 def split(x):
@@ -218,10 +229,8 @@
     return jnp.concatenate([weight[0:1, :], weight[1:2, :]] * (tiles // 2), axis=1)
 
 
-def image_kernel(basis_ref, weight_ref, level_ref, matrix, inverse_ref, image_ref):
-    total = basis_ref.shape[1]
-    level = level_ref[...]
-    weight = unknown_weights(weight_ref[...], total // TILE)
+def sketch(basis, weight, level, matrix, careful):
+    total = basis.shape[1]
     step_weight = weight * (1.0 / SHIFT)
 
     def image_of(basis):
@@ -236,41 +245,19 @@
     def normaliser(image):
         return eliminate(dot_nt(image, image, HIGHEST) * (1.0 / total))
 
-    image = basis_ref[...]
-    for _ in range(ITERS):
-        image = image_of(image)
-    inverse, least = normaliser(image)
-    inverse_ref[...] = inverse
-    image_ref[...] = image
-
-    @pl.when(jnp.logical_not(least > SAFE_PIVOT))
-    def _():
-        def iteration(_, basis):
-            image = image_of(basis)
-            inverse, _ = normaliser(image)
-            return jnp.dot(inverse, image, preferred_element_type=F32, precision=HIGHEST)
-
-        basis = lax.fori_loop(0, ITERS - 1, iteration, basis_ref[...])
+    def iteration(_, basis):
         image = image_of(basis)
         inverse, _ = normaliser(image)
-        inverse_ref[...] = inverse
-        image_ref[...] = image
-
-
-def last_image(basis, weight, level, matrix):
-    probes = basis.shape[0]
-    vmem = pl.BlockSpec(memory_space=pltpu.VMEM)
-    return pl.pallas_call(
-        image_kernel,
-        out_shape=(
-            jax.ShapeDtypeStruct((probes, probes), F32),
-            jax.ShapeDtypeStruct(basis.shape, F32),
-        ),
-        in_specs=[vmem] * 4,
-        out_specs=(vmem, vmem),
-        compiler_params=pltpu.CompilerParams(vmem_limit_bytes=24 * 2**20),
-        name="last_image",
-    )(basis, weight, level, matrix)
+        return jnp.dot(inverse, image, preferred_element_type=F32, precision=HIGHEST)
+
+    if careful:
+        image = image_of(lax.fori_loop(0, ITERS - 1, iteration, basis))
+    else:
+        image = basis
+        for _ in range(ITERS):
+            image = image_of(image)
+    inverse, safe = normaliser(image)
+    return image, inverse, safe
 
 
 PLANE = 9
@@ -317,19 +304,29 @@
     return jnp.where(r < DEFL, m * DEFL + r, ends)
 
 
+def group_order(i):
+    tiles = ROW_GROUPS * DEFL // TILE
+    return i % tiles * (TILE // DEFL) + i // tiles
+
+
 def line_tree():
     side = [(0, 5), (0, 2), (2, 1), (2, 3), (5, 4), (5, 6), (5, 7)]
     return side + [(-a, -b) for a, b in side] + [(5, 8)]
 
 
 def exchange_kernel(
-    inverse_ref, image_ref, weight_ref, level_ref, matrix_ref,
-    out_ref, defl_ref,
-    field_ref, full, sides, line_slots, wide_ref, send_sem, recv_sem, line_send, line_recv,
+    careful,
+    basis_ref, weight_ref, level_ref, matrix_ref,
+    out_ref, defl_ref, safe_ref,
+    field_ref, full, sides, line_slots, wide_ref, safe_x, safe_y, safe_z,
+    send_sem, recv_sem, line_send, line_recv, x_send, x_recv, y_send, y_recv,
+    z_send, z_recv,
 ):
     n_x, n_y, n_z = (lax.axis_size(a) for a in ("gx", "gy", "gz"))
     my_x, my_y, my_z = (lax.axis_index(a) for a in ("gx", "gy", "gz"))
-    half = field_ref.shape[2]
+    total = basis_ref.shape[1]
+    tiles = total // TILE
+    half = total // 2
     tree = line_tree()
 
     def device(m):
@@ -339,27 +336,31 @@
     def line(step):
         return (my_x, my_y, lax.rem(my_z + step + n_z, n_z))
 
+    def row_x(step):
+        return (lax.rem(my_x + step, n_x), my_y, my_z)
+
+    def row_y(step):
+        return (my_x, lax.rem(my_y + step, n_y), my_z)
+
     neighbours = [m for m in range(PLANE) if m != OWN]
-    distances = sorted({abs(b - a) for a, b in tree})
     barrier = pltpu.get_barrier_semaphore()
-    for distance in reversed(distances):
-        for step in (-distance, distance):
-            pl.semaphore_signal(barrier, inc=1, device_id=line(step), device_id_type=MESH)
-    for m in neighbours:
-        pl.semaphore_signal(barrier, inc=1, device_id=device(m), device_id_type=MESH)
-
-    total = image_ref.shape[1]
-    tiles = total // TILE
-    basis = jnp.dot(
-        inverse_ref[...], image_ref[...], preferred_element_type=F32, precision=HIGHEST
-    )
+    for step in sorted(range(1, n_z), key=lambda step: -min(step, n_z - step)):
+        pl.semaphore_signal(barrier, inc=1, device_id=line(step), device_id_type=MESH)
+    others = [row_x(step) for step in range(2, n_x - 1)] + [row_y(step) for step in range(2, n_y - 1)]
+    for there in others + [device(m) for m in neighbours]:
+        pl.semaphore_signal(barrier, inc=1, device_id=there, device_id_type=MESH)
+
+    weight = unknown_weights(weight_ref[...], tiles)
+    image, inverse, safe = sketch(basis_ref[...], weight, level_ref[...], matrix_ref, careful)
+    safe_x[0:1, :] = jnp.concatenate([safe, safe], axis=1)[:, :TILE]
+    basis = jnp.dot(inverse, image, preferred_element_type=F32, precision=HIGHEST)
     kept = basis[:DEFL]
-    weighted = (kept * unknown_weights(weight_ref[...], tiles)).astype(BF16)
+    weighted = (kept * weight).astype(BF16)
     for t in range(tiles):
         field_ref[t % 2, :, t // 2 * TILE : (t // 2 + 1) * TILE] = weighted[
             :, t * TILE : (t + 1) * TILE
         ]
-    pl.semaphore_wait(barrier, len(neighbours) + 2 * len(distances))
+    pl.semaphore_wait(barrier, len(others) + len(neighbours) + n_z - 1)
 
     slot = {m: i for i, m in enumerate(m for m in neighbours if plane_step(m)[1] != 0)}
     copies = []
@@ -381,6 +382,23 @@
         copy.start()
         copies.append(copy)
 
+    def spread_safe(rows, count, where, sends, recvs):
+        out = []
+        for step in range(1, count):
+            copy = pltpu.make_async_remote_copy(
+                src_ref=rows.at[pl.ds(0, 1)],
+                dst_ref=rows.at[pl.ds(step, 1)],
+                send_sem=sends.at[step],
+                recv_sem=recvs.at[step],
+                device_id=where(step),
+                device_id_type=MESH,
+            )
+            copy.start()
+            out.append(copy)
+        return out
+
+    safe_copies = spread_safe(safe_x, n_x, row_x, x_send, x_recv)
+
     for t in range(tiles):
         wide_ref[pl.ds(t, DEFL, stride=tiles), :] = kept[:, t * TILE : (t + 1) * TILE]
     defl_ref[...] = wide_ref[...].astype(BF16)
@@ -392,14 +410,18 @@
     pick = [end_picker(y, half) for y in range(2)]
     own = [field_ref[y] for y in range(2)]
     stack = [[jnp.concatenate([-own[y], pick[z]], axis=0) for z in range(2)] for y in range(2)]
-    lanes = PAYLOAD_LANES
-    spread = (iota((DEFL, lanes), 1) % DEFL == iota((DEFL, lanes), 0)).astype(BF16)
     rows = PLANE * (DEFL + PARTS)
-    place = payload_group(iota((rows, 1), 0)) % ROW_GROUPS
-    keep = iota((rows, lanes), 1) // DEFL == place
-    target = payload_group(iota((PAYLOAD_ROWS, rows), 1))
-    gather = (target >= 0) & (target // ROW_GROUPS == iota((PAYLOAD_ROWS, rows), 0))
-    gather = gather.astype(BF16)
+    per_tile = TILE // DEFL
+    groups = PAYLOAD_ROWS * ROW_GROUPS
+    order = iota((groups, 1), 0)
+    order = modulo(order, PAYLOAD_ROWS) * ROW_GROUPS + group_order(over(order, PAYLOAD_ROWS))
+    arrange = (payload_group(iota((1, rows), 1)) == order).astype(BF16)
+    lane, value = iota((DEFL, TILE), 1), iota((DEFL, TILE), 0)
+    place = [(lane == value + v * DEFL).astype(BF16) for v in range(per_tile)]
+    for copy in safe_copies:
+        copy.wait_recv()
+    safe_y[0:1, :] = jnp.min(safe_x[...], axis=0, keepdims=True)
+    safe_copies += spread_safe(safe_y, n_y, row_y, y_send, y_recv)
     for copy in copies:
         copy.wait_recv()
 
@@ -425,9 +447,18 @@
         parts.append(jnp.where(inside, block, 0.0))
     parts = jnp.concatenate(parts, axis=0).astype(BF16)
 
-    wide = jnp.dot(parts, spread, preferred_element_type=F32)
-    wide = jnp.where(keep, wide, 0.0).astype(BF16)
-    line_slots[my_z] = jnp.dot(gather, wide, preferred_element_type=F32).astype(BF16)
+    sorted_rows = jnp.dot(arrange, parts, preferred_element_type=F32).astype(BF16)
+    count = groups // per_tile
+    flat = sum(
+        jnp.dot(
+            sorted_rows[v * count : (v + 1) * count], place[v], preferred_element_type=F32
+        )
+        for v in range(per_tile)
+    ).astype(BF16)
+    for i in range(ROW_GROUPS // per_tile):
+        line_slots[my_z, :, i * TILE : (i + 1) * TILE] = flat[
+            i * PAYLOAD_ROWS : (i + 1) * PAYLOAD_ROWS
+        ]
 
     sign = 1 - 2 * lax.rem(my_x, 2)
     hops = {}
@@ -448,6 +479,10 @@
     for parent, child in tree:
         if parent == 0:
             send(parent, child)
+    for copy in safe_copies[n_x - 1 :]:
+        copy.wait_recv()
+    safe_z[0:1, :] = jnp.min(safe_y[...], axis=0, keepdims=True)
+    safe_copies_z = spread_safe(safe_z, n_z, line, z_send, z_recv)
     parents = [p for p in sorted({p for p, _ in tree}, key=abs) if p != 0]
     for p in parents:
         hops[p].wait_recv()
@@ -457,41 +492,57 @@
     for child, hop in hops.items():
         if child not in parents:
             hop.wait_recv()
-    for copy in copies + list(hops.values()):
+    for copy in safe_copies_z:
+        copy.wait_recv()
+    for copy in copies + safe_copies + safe_copies_z + list(hops.values()):
         copy.wait_send()
     out_ref[...] = line_slots[...]
-
-
-def exchange(inverse, image, weight, level, matrix, n_z):
+    safe_ref[...] = jnp.min(safe_z[...], axis=0, keepdims=True)
+
+
+def exchange(basis, weight, level, matrix, sizes, careful):
     vmem = pl.BlockSpec(memory_space=pltpu.VMEM)
     dma = pltpu.SemaphoreType.DMA
-    total = image.shape[1]
+    n_x, n_y, n_z = sizes
+    total = basis.shape[1]
     payload = (n_z, PAYLOAD_ROWS, PAYLOAD_LANES)
     rows = DEFL * total // TILE
     return pl.pallas_call(
-        exchange_kernel,
+        functools.partial(exchange_kernel, careful),
         out_shape=(
             jax.ShapeDtypeStruct(payload, BF16),
             jax.ShapeDtypeStruct((rows, TILE), BF16),
+            jax.ShapeDtypeStruct((1, TILE), F32),
         ),
-        in_specs=[vmem] * 5,
-        out_specs=(vmem, vmem),
+        in_specs=[vmem] * 4,
+        out_specs=(vmem, vmem, vmem),
         scratch_shapes=[
             pltpu.VMEM((2, DEFL, total // 2), BF16),
             pltpu.VMEM((2, 2, DEFL, total // 2), BF16),
             pltpu.VMEM((6, DEFL, total // 2), BF16),
             pltpu.VMEM(payload, BF16),
             pltpu.VMEM((rows, TILE), F32),
+            pltpu.VMEM((n_x, TILE), F32),
+            pltpu.VMEM((n_y, TILE), F32),
+            pltpu.VMEM((n_z, TILE), F32),
             dma((PLANE,)),
             dma((PLANE,)),
             dma((n_z + 1,)),
             dma((n_z + 1,)),
+            dma((n_x,)),
+            dma((n_x,)),
+            dma((n_y,)),
+            dma((n_y,)),
+            dma((n_z,)),
+            dma((n_z,)),
         ],
         compiler_params=pltpu.CompilerParams(
-            collective_id=1, has_side_effects=True, vmem_limit_bytes=24 * 2**20
+            collective_id=2 if careful else 1,
+            has_side_effects=True,
+            vmem_limit_bytes=24 * 2**20,
         ),
-        name="exchange",
-    )(inverse, image, weight, level, matrix)
+        name="exchange_careful" if careful else "exchange",
+    )(basis, weight, level, matrix)
 
 
 def pair_index(m, step_z):
@@ -521,9 +572,9 @@
 
     def select(first, count, shift):
         index = iota((count * n_z, 1), 0)
-        member = index % n_z + shift
+        member = modulo(index, n_z) + shift
         inside = (member >= 0) & (member < n_z)
-        wanted = jnp.where(inside, member * PAYLOAD_ROWS + first + index // n_z, -1)
+        wanted = jnp.where(inside, member * PAYLOAD_ROWS + first + over(index, n_z), -1)
         hit = (column == wanted).astype(BF16)
         return jnp.dot(hit, packed, preferred_element_type=F32)
 
@@ -559,10 +610,10 @@
         [tile_of(rows, end * end_tiles + own_first + i) for end in range(2) for i in range(own_count)],
         axis=0,
     )
-    value, lane = iota((TILE, width), 0), iota((TILE, width), 1)
+    distance = iota((TILE, width), 0) - over(iota((TILE, width), 1), DEFL)
     own = []
     for v in range(per_tile):
-        spread = jnp.where(value == v * DEFL + lane // DEFL, -1.0, 0.0).astype(BF16)
+        spread = jnp.where(distance == v * DEFL, -1.0, 0.0).astype(BF16)
         own.append(jnp.dot(own_tiles, spread, preferred_element_type=F32))
 
     def own_part(end, y, c):
@@ -571,7 +622,7 @@
         return own[group % per_tile][start : start + n_z]
 
     value, lane = iota((TILE, per_tile * TILE), 0), iota((TILE, per_tile * TILE), 1)
-    repeat = (value == lane // TILE * DEFL + lane % DEFL).astype(BF16)
+    repeat = (value == over(lane, TILE) * DEFL + modulo(lane, DEFL)).astype(BF16)
     for step_z in (-1, 1):
         their_end, own_end = (0, 1) if step_z > 0 else (1, 0)
         rows = select(block_rows, end_rows, step_z).astype(BF16)
@@ -619,7 +670,8 @@
 
 
 def per_device(probes, stiffness, diag_tiles, off_tiles, off_rows, off_cols, off_count):
-    n_z = lax.axis_size("gz")
+    sizes = tuple(lax.axis_size(a) for a in ("gx", "gy", "gz"))
+    n_z = sizes[2]
     cell_shape = probes.shape[1:]
     weight, basis, level, matrix = sketch_operands(
         probes.reshape(-1, TILE),
@@ -630,9 +682,15 @@
         off_cols[0, 0, 0],
         off_count[0, 0],
     )
-    inverse, image = last_image(basis, weight, level, matrix)
-    gathered, kept = exchange(inverse, image, weight, level, matrix, n_z)
-    coarse_self, coarse_pairs, deflation = unpack(gathered, kept, n_z)
+    gathered, kept, safe = exchange(basis, weight, level, matrix, sizes, careful=False)
+
+    def careful():
+        again = exchange(basis, weight, level, matrix, sizes, careful=True)
+        return unpack(again[0], again[1], n_z)
+
+    coarse_self, coarse_pairs, deflation = lax.cond(
+        safe[0, 0] > 0.5, lambda: unpack(gathered, kept, n_z), careful
+    )
     return (
         deflation.reshape((DEFL,) + cell_shape),
         coarse_self[None, None],

time: 47.9 us -> 45.1 us (0.942); the launches traced: 47.7 us -> 44.4 us
  Pallas kernels: 46.4 us -> 43 us
    pallas_call x2 -> x1, Pallas kernels: 29.2 us -> 25.8 us  [exchange(): pl.pallas_call(functools.partial(exchange_kernel, careful), out_shape=(ja...]
where the time goes in v3:
time: 45.1 us; the launch traced here: 44.4 us
  Pallas kernels  43 us (95%)
  between operations  1.33 us (3%)
    pallas_call x1, Pallas kernels, exchange(): pl.pallas_call(functools.partial(exchange_kernel, careful), out_shape=(ja...  25.8 us
    pallas_call x1, Pallas kernels, sketch_operands(): pl.pallas_call(operands_kernel, out_shape=(jax.ShapeDtypeStruct(stiff.sha...  15.1 us
    pallas_call x1, Pallas kernels, unpack(): pl.pallas_call(unpack_kernel, out_shape=(jax.ShapeDtypeStruct((n_z, width...  2.11 us

profile of v3, /device:TPU:1, one launch (start us, length us, event | category | flops | bytes accessed | tf_op | source)
XLA Modules:
  0.0 44.4 jit_solution(14731379778193154912)
XLA Ops:
  1.3 15.1 %sketch_operands.1 = (f32[2,128]{1,0:T(2,128)S(1)}, f32[48,768]{1,0:T(8,128)S(1)}, f32[1,768]{1,0:T(1,128)S(1)}, bf16[768,768]{1,0:T(8,128)(2,1)S(1)}) custom-call(f32[2,128]{1,0:T(2,128)} %bitcast.27, s32[24]{0:T(128)} %bitcast.28, s32[24]{0:T(128)} %bitcast.29, s32[1]{0:T(128)} %bitcast.20.count_hbm, bf16[288,128]{1,0:T(8,128)(2,1)} %bitcast.26, ...), custom_call_target="tpu_custom_call" | custom-call | tf_op jit(solution)/shard_map/sketch_operands/pallas_call | solution.py:162
  16.4 25.8 %exchange.1 = (bf16[16,16,768]{2,1,0:T(8,128)(2,1)S(1)}, bf16[192,128]{1,0:T(8,128)(2,1)S(1)}, f32[1,128]{1,0:T(1,128)S(1)}) custom-call(f32[48,768]{1,0:T(8,128)S(1)} %get-tuple-element.47.basis_ref, f32[2,128]{1,0:T(2,128)S(1)} %get-tuple-element.48.weight_ref, f32[1,768]{1,0:T(1,128)S(1)} %get-tuple-element.49.level_ref, ...), custom_call_target="tpu_custom_call" | custom-call | tf_op jit(solution)/shard_map/exchange/pallas_call | solution.py:510
  42.2 2.1 %conditional.1 = ((f32[16,1024]{1,0:T(8,128)}, f32[26,16,1024]{2,1,0:T(8,128)}, bf16[192,128]{1,0:T(8,128)(2,1)})) conditional(s32[]{:T(128)} %bitcast.9, (f32[48,768]{1,0:T(8,128)S(1)}, f32[2,128]{1,0:T(2,128)S(1)}, f32[1,768]{1,0:T(1,128)S(1)}, bf16[768,768]{1,0:T(8,128)(2,1)S(1)}) %tuple.20, (bf16[16,16,768]{2,1,0:T(8,128)(2,1)S(1)}, ...), branch_computations={%region_0.0_spmd.clone, %region_1.0_spmd.clone} | conditional | bytes 8 | solution.py:691
  42.3 2.1 %unpack.3 = (f32[16,1024]{1,0:T(8,128)}, f32[26,16,1024]{2,1,0:T(8,128)}, bf16[192,128]{1,0:T(8,128)(2,1)}) custom-call(bf16[256,768]{1,0:T(8,128)(2,1)S(1)} %bitcast.24, bf16[192,128]{1,0:T(8,128)(2,1)S(1)} %get-tuple-element.73.kept_ref), custom_call_target="tpu_custom_call" | custom-call | tf_op jit(solution)/shard_map/cond/branch_1_fun/unpack/pallas_call | solution.py:653

commit v4 on v3

--- a/solution.py
+++ b/solution.py
@@ -344,7 +344,8 @@
 
     neighbours = [m for m in range(PLANE) if m != OWN]
     barrier = pltpu.get_barrier_semaphore()
-    for step in sorted(range(1, n_z), key=lambda step: -min(step, n_z - step)):
+    distances = sorted({abs(child - parent) for parent, child in tree}, reverse=True)
+    for step in [sign * distance for distance in distances for sign in (-1, 1)]:
         pl.semaphore_signal(barrier, inc=1, device_id=line(step), device_id_type=MESH)
     others = [row_x(step) for step in range(2, n_x - 1)] + [row_y(step) for step in range(2, n_y - 1)]
     for there in others + [device(m) for m in neighbours]:
@@ -360,10 +361,10 @@
         field_ref[t % 2, :, t // 2 * TILE : (t // 2 + 1) * TILE] = weighted[
             :, t * TILE : (t + 1) * TILE
         ]
-    pl.semaphore_wait(barrier, len(others) + len(neighbours) + n_z - 1)
+    pl.semaphore_wait(barrier, len(others) + len(neighbours) + 2 * len(distances))
 
     slot = {m: i for i, m in enumerate(m for m in neighbours if plane_step(m)[1] != 0)}
-    copies = []
+    copies, arrival = [], {}
     for m in neighbours:
         step_x, step_y = plane_step(m)
         back = PLANE - 1 - m
@@ -381,6 +382,7 @@
         )
         copy.start()
         copies.append(copy)
+        arrival[back] = copy
 
     def spread_safe(rows, count, where, sends, recvs):
         out = []
@@ -418,20 +420,16 @@
     arrange = (payload_group(iota((1, rows), 1)) == order).astype(BF16)
     lane, value = iota((DEFL, TILE), 1), iota((DEFL, TILE), 0)
     place = [(lane == value + v * DEFL).astype(BF16) for v in range(per_tile)]
+    blocks = {}
+    ends = dot_nt(pick[0], own[0]) + dot_nt(pick[1], own[1])
+    blocks[OWN] = jnp.concatenate([self_block, ends], axis=0)
     for copy in safe_copies:
         copy.wait_recv()
     safe_y[0:1, :] = jnp.min(safe_x[...], axis=0, keepdims=True)
     safe_copies += spread_safe(safe_y, n_y, row_y, y_send, y_recv)
-    for copy in copies:
-        copy.wait_recv()
-
-    parts = []
-    for m in range(PLANE):
+    for m in sorted(neighbours, key=lambda m: sum(map(abs, plane_step(m)))):
         step_x, step_y = plane_step(m)
-        if m == OWN:
-            ends = dot_nt(pick[0], own[0]) + dot_nt(pick[1], own[1])
-            parts.append(jnp.concatenate([self_block, ends], axis=0))
-            continue
+        arrival[m].wait_recv()
         if step_y == 0:
             side = m // 3 // 2
             block = dot_nt(stack[0][0], full[side, 0]) + dot_nt(stack[1][1], full[side, 1])
@@ -444,8 +442,8 @@
             inside = my_x < n_x - 1 if step_x > 0 else my_x > 0
         if step_y != 0:
             inside = jnp.logical_and(inside, my_y < n_y - 1 if step_y > 0 else my_y > 0)
-        parts.append(jnp.where(inside, block, 0.0))
-    parts = jnp.concatenate(parts, axis=0).astype(BF16)
+        blocks[m] = jnp.where(inside, block, 0.0)
+    parts = jnp.concatenate([blocks[m] for m in range(PLANE)], axis=0).astype(BF16)
 
     sorted_rows = jnp.dot(arrange, parts, preferred_element_type=F32).astype(BF16)
     count = groups // per_tile
@@ -461,40 +459,41 @@
         ]
 
     sign = 1 - 2 * lax.rem(my_x, 2)
-    hops = {}
-
-    def send(parent, child):
-        owner = line_slots.at[lax.rem(my_z - sign * parent + n_z, n_z)]
-        hop = pltpu.make_async_remote_copy(
-            src_ref=owner,
-            dst_ref=owner,
-            send_sem=line_send.at[child + n_z // 2],
-            recv_sem=line_recv.at[child + n_z // 2],
-            device_id=line(sign * (child - parent)),
-            device_id_type=MESH,
-        )
-        hop.start()
-        hops[child] = hop
-
-    for parent, child in tree:
-        if parent == 0:
-            send(parent, child)
+    parents = sorted({parent for parent, _ in tree} - {0}, key=abs)
+
+    def send(slots, parent, sends, recvs):
+        hops = {}
+        for start, child in tree:
+            if start != parent:
+                continue
+            owner = slots.at[pl.ds(lax.rem(my_z - sign * parent + n_z, n_z), 1)]
+            hops[child] = pltpu.make_async_remote_copy(
+                src_ref=owner,
+                dst_ref=owner,
+                send_sem=sends.at[child + n_z // 2],
+                recv_sem=recvs.at[child + n_z // 2],
+                device_id=line(sign * (child - parent)),
+                device_id_type=MESH,
+            )
+            hops[child].start()
+        return hops
+
+    hops = send(line_slots, 0, line_send, line_recv)
     for copy in safe_copies[n_x - 1 :]:
         copy.wait_recv()
-    safe_z[0:1, :] = jnp.min(safe_y[...], axis=0, keepdims=True)
-    safe_copies_z = spread_safe(safe_z, n_z, line, z_send, z_recv)
-    parents = [p for p in sorted({p for p, _ in tree}, key=abs) if p != 0]
-    for p in parents:
-        hops[p].wait_recv()
-        for parent, child in tree:
-            if parent == p:
-                send(parent, child)
-    for child, hop in hops.items():
-        if child not in parents:
-            hop.wait_recv()
-    for copy in safe_copies_z:
-        copy.wait_recv()
-    for copy in copies + safe_copies + safe_copies_z + list(hops.values()):
+    safe_z[pl.ds(my_z, 1), :] = jnp.min(safe_y[...], axis=0, keepdims=True)
+    safe_hops = send(safe_z, 0, z_send, z_recv)
+    for parent in parents:
+        hops[parent].wait_recv()
+        hops.update(send(line_slots, parent, line_send, line_recv))
+    for parent in parents:
+        safe_hops[parent].wait_recv()
+        safe_hops.update(send(safe_z, parent, z_send, z_recv))
+    for copies_of in (hops, safe_hops):
+        for child, copy in copies_of.items():
+            if child not in parents:
+                copy.wait_recv()
+    for copy in copies + safe_copies + list(hops.values()) + list(safe_hops.values()):
         copy.wait_send()
     out_ref[...] = line_slots[...]
     safe_ref[...] = jnp.min(safe_z[...], axis=0, keepdims=True)
@@ -533,8 +532,8 @@
             dma((n_x,)),
             dma((n_y,)),
             dma((n_y,)),
-            dma((n_z,)),
-            dma((n_z,)),
+            dma((n_z + 1,)),
+            dma((n_z + 1,)),
         ],
         compiler_params=pltpu.CompilerParams(
             collective_id=2 if careful else 1,
@@ -570,16 +569,25 @@
     packed = gathered_ref[...]
     column = iota((1, n_z * PAYLOAD_ROWS), 1)
 
-    def select(first, count, shift):
+    def hits(first, count, shift):
         index = iota((count * n_z, 1), 0)
         member = modulo(index, n_z) + shift
         inside = (member >= 0) & (member < n_z)
         wanted = jnp.where(inside, member * PAYLOAD_ROWS + first + over(index, n_z), -1)
-        hit = (column == wanted).astype(BF16)
-        return jnp.dot(hit, packed, preferred_element_type=F32)
+        return (column == wanted).astype(BF16)
 
     block_rows = BLOCK_GROUPS // ROW_GROUPS
-    rows = select(0, block_rows, 0)
+    end_rows = 2 * END_GROUPS // ROW_GROUPS
+    wanted = [hits(0, block_rows, 0)] + [hits(block_rows, end_rows, step) for step in (0, -1, 1)]
+    selected = jnp.dot(
+        jnp.concatenate(wanted, axis=0), packed, preferred_element_type=F32
+    )
+    rows = selected[: block_rows * n_z]
+
+    def ends_of(i):
+        start = (block_rows + i * end_rows) * n_z
+        return selected[start : start + end_rows * n_z].astype(BF16)
+
     for m in range(PLANE):
         pieces, group = [], m * DEFL
         while group < (m + 1) * DEFL:
@@ -597,7 +605,6 @@
     per_tile = TILE // DEFL
     row_tiles = ROW_GROUPS // per_tile
     end_tiles = END_GROUPS // per_tile
-    end_rows = 2 * END_GROUPS // ROW_GROUPS
 
     def tile_of(rows, number):
         row, i = number // row_tiles, number % row_tiles
@@ -605,7 +612,7 @@
 
     own_first = end_group(OWN, 0, 0) // per_tile
     own_count = end_group(OWN, 1, 2) // per_tile + 1 - own_first
-    rows = select(block_rows, end_rows, 0).astype(BF16)
+    rows = ends_of(0)
     own_tiles = jnp.concatenate(
         [tile_of(rows, end * end_tiles + own_first + i) for end in range(2) for i in range(own_count)],
         axis=0,
@@ -625,7 +632,7 @@
     repeat = (value == over(lane, TILE) * DEFL + modulo(lane, DEFL)).astype(BF16)
     for step_z in (-1, 1):
         their_end, own_end = (0, 1) if step_z > 0 else (1, 0)
-        rows = select(block_rows, end_rows, step_z).astype(BF16)
+        rows = ends_of(1 if step_z < 0 else 2)
         tiles = [tile_of(rows, their_end * end_tiles + i) for i in range(end_tiles)]
         theirs = jnp.dot(jnp.concatenate(tiles, axis=0), repeat, preferred_element_type=F32)
         for m in range(PLANE):

time: 45.1 us -> 45.1 us (level)
  the two profiles are of different devices: /device:TPU:1 before, /device:TPU:4 now
where the time goes in v4:
time: 45.1 us; the launch traced here: 44.9 us
  Pallas kernels  43.6 us (97%)
  between operations  1.33 us (3%)
    pallas_call x1, Pallas kernels, exchange(): pl.pallas_call(functools.partial(exchange_kernel, careful), out_shape=(ja...  26.1 us
    pallas_call x1, Pallas kernels, sketch_operands(): pl.pallas_call(operands_kernel, out_shape=(jax.ShapeDtypeStruct(stiff.sha...  15.4 us
    pallas_call x1, Pallas kernels, unpack(): pl.pallas_call(unpack_kernel, out_shape=(jax.ShapeDtypeStruct((n_z, width...  2.02 us

profile of v4, /device:TPU:4, one launch (start us, length us, event | category | flops | bytes accessed | tf_op | source)
XLA Modules:
  0.0 44.9 jit_solution(14263586583156642463)
XLA Ops:
  1.3 15.4 %sketch_operands.1 = (f32[2,128]{1,0:T(2,128)S(1)}, f32[48,768]{1,0:T(8,128)S(1)}, f32[1,768]{1,0:T(1,128)S(1)}, bf16[768,768]{1,0:T(8,128)(2,1)S(1)}) custom-call(f32[2,128]{1,0:T(2,128)} %bitcast.27, s32[24]{0:T(128)} %bitcast.28, s32[24]{0:T(128)} %bitcast.29, s32[1]{0:T(128)} %bitcast.20.count_hbm, bf16[288,128]{1,0:T(8,128)(2,1)} %bitcast.26, ...), custom_call_target="tpu_custom_call" | custom-call | tf_op jit(solution)/shard_map/sketch_operands/pallas_call | solution.py:162
  16.7 26.1 %exchange.1 = (bf16[16,16,768]{2,1,0:T(8,128)(2,1)S(1)}, bf16[192,128]{1,0:T(8,128)(2,1)S(1)}, f32[1,128]{1,0:T(1,128)S(1)}) custom-call(f32[48,768]{1,0:T(8,128)S(1)} %get-tuple-element.47.basis_ref, f32[2,128]{1,0:T(2,128)S(1)} %get-tuple-element.48.weight_ref, f32[1,768]{1,0:T(1,128)S(1)} %get-tuple-element.49.level_ref, ...), custom_call_target="tpu_custom_call" | custom-call | tf_op jit(solution)/shard_map/exchange/pallas_call | solution.py:509
  42.9 2.0 %conditional.1 = ((f32[16,1024]{1,0:T(8,128)}, f32[26,16,1024]{2,1,0:T(8,128)}, bf16[192,128]{1,0:T(8,128)(2,1)})) conditional(s32[]{:T(128)} %bitcast.9, (f32[48,768]{1,0:T(8,128)S(1)}, f32[2,128]{1,0:T(2,128)S(1)}, f32[1,768]{1,0:T(1,128)S(1)}, bf16[768,768]{1,0:T(8,128)(2,1)S(1)}) %tuple.20, (bf16[16,16,768]{2,1,0:T(8,128)(2,1)S(1)}, ...), branch_computations={%region_0.0_spmd.clone, %region_1.0_spmd.clone} | conditional | bytes 8 | solution.py:698
  42.9 2.0 %unpack.3 = (f32[16,1024]{1,0:T(8,128)}, f32[26,16,1024]{2,1,0:T(8,128)}, bf16[192,128]{1,0:T(8,128)(2,1)}) custom-call(bf16[256,768]{1,0:T(8,128)(2,1)S(1)} %bitcast.24, bf16[192,128]{1,0:T(8,128)(2,1)S(1)} %get-tuple-element.73.kept_ref), custom_call_target="tpu_custom_call" | custom-call | tf_op jit(solution)/shard_map/cond/branch_1_fun/unpack/pallas_call | solution.py:660
